TPU v7x, 32 devices: a whole 2x2x4 slice. The times are simulated.
32 devices in a mesh: fsdp: 2 (over x), dp: 16 (over z, y, core).
Axes of the slice: x: 2, y: 2, z: 4, core: 2. Of those that a mesh axis runs over, the one named last changes fastest.
Arguments:
- hidden_in: bfloat16 [64, 512, 768], P(('fsdp', 'dp')), may hold values from -6 to 6
- lengths: int32 [64], P(('fsdp', 'dp')), may hold values from 1 to 512, 17920 in all
- query_w: bfloat16 [768, 768], P('fsdp'), may hold values from -0.21875 to 0.21875
- key_w: bfloat16 [768, 768], P('fsdp'), may hold values from -0.21875 to 0.21875
- value_w: bfloat16 [768, 768], P('fsdp'), may hold values from -0.21875 to 0.21875
- out_w: bfloat16 [768, 768], P('fsdp'), may hold values from -1.75 to 1.75
- query_b: bfloat16 [768], P('fsdp'), may hold values from -3 to 3
- value_b: bfloat16 [768], P('fsdp'), may hold values from -3 to 3
- out_b: bfloat16 [768], P('fsdp'), may hold values from -3 to 3
- gain_one: bfloat16 [768], P('fsdp'), may hold values from 0.5 to 1.5
- shift_one: bfloat16 [768], P('fsdp'), may hold values from -3 to 3
- up_w: bfloat16 [768, 3072], P('fsdp'), may hold values from -0.21875 to 0.21875
- up_b: bfloat16 [3072], P('fsdp'), may hold values from -3 to 3
- down_w: bfloat16 [3072, 768], P('fsdp'), may hold values from -0.109375 to 0.109375
- down_b: bfloat16 [768], P('fsdp'), may hold values from -3 to 3
- gain_two: bfloat16 [768], P('fsdp'), may hold values from 0.5 to 1.5
- shift_two: bfloat16 [768], P('fsdp'), may hold values from -3 to 3
- cotangent: bfloat16 [64, 512, 768], P(('fsdp', 'dp')), may hold values from -6 to 6
Outputs:
- block_out: bfloat16 [64, 512, 768], P(('fsdp', 'dp'))
- grad_in: float32 [64, 512, 768], P(('fsdp', 'dp'))
- grad_query_w: float32 [768, 768], P('fsdp')
- grad_key_w: float32 [768, 768], P('fsdp')
- grad_value_w: float32 [768, 768], P('fsdp')
- grad_out_w: float32 [768, 768], P('fsdp')
- grad_query_b: float32 [768], P('fsdp')
- grad_value_b: float32 [768], P('fsdp')
- grad_out_b: float32 [768], P('fsdp')
- grad_gain_one: float32 [768], P('fsdp')
- grad_shift_one: float32 [768], P('fsdp')
- grad_up_w: float32 [768, 3072], P('fsdp')
- grad_up_b: float32 [3072], P('fsdp')
- grad_down_w: float32 [3072, 768], P('fsdp')
- grad_down_b: float32 [768], P('fsdp')
- grad_gain_two: float32 [768], P('fsdp')
- grad_shift_two: float32 [768], P('fsdp')
Inputs may be any that keep to these rules, and one draw needn't show every extreme that they name: `lengths`: the longest sequence of the whole batch has exactly 512 real tokens.
All inputs are finite; a program needn't handle non-finite values. No bound on the sum of `lengths` on one device may be relied on, other than what follows from the above.
Results may differ from a plain program's by a relative error of at most 0.014.
Values may be sent and summed in bfloat16 or wider, within the bound.
A program may use at most 192 MiB of HBM per device.

v0:
```python
import math

import jax
import jax.numpy as jnp
from jax import lax
from jax.sharding import PartitionSpec as P

HEADS = 12


norm_eps = 1e-12
mask_fill = -1e30


def product(left, right):
    return jnp.dot(left, right, preferred_element_type=jnp.float32)


def trans_left(left, right):
    return lax.dot_general(
        left, right, (((0,), (0,)), ((), ())), preferred_element_type=jnp.float32
    )


def trans_right(left, right):
    return lax.dot_general(
        left, right, (((1,), (1,)), ((), ())), preferred_element_type=jnp.float32
    )


def normalize(summed):
    average = jnp.mean(summed, axis=-1, keepdims=True)
    centred = summed - average
    inverse = lax.rsqrt(jnp.mean(centred * centred, axis=-1, keepdims=True) + norm_eps)
    return (centred * inverse, inverse)


def norm_back(grad_normed, normed, inverse):
    first_mean = jnp.mean(grad_normed, axis=-1, keepdims=True)
    cross_mean = jnp.mean(grad_normed * normed, axis=-1, keepdims=True)
    return inverse * (grad_normed - first_mean - normed * cross_mean)


def masked_scores(query_vectors, key_vectors, length):
    score_scale = 1.0 / math.sqrt(query_vectors.shape[-1])
    unmasked_score_matrix = (
        jnp.einsum("gyx,uyx->ygu", query_vectors, key_vectors, preferred_element_type=jnp.float32)
        * score_scale
    )
    allowed = jnp.arange(key_vectors.shape[0], dtype=jnp.int32) < length
    return (jnp.where(allowed[None, None, :], unmasked_score_matrix, mask_fill), score_scale)


def attend_one(item):
    query_vectors, key_vectors, value_vectors, length = item
    scores, score_scale = masked_scores(query_vectors, key_vectors, length)
    precision_highest = jnp.max(scores, axis=-1, keepdims=True)
    exponent = jnp.exp(scores - precision_highest)
    totals = jnp.sum(exponent, axis=-1, keepdims=True)
    attention_probs = exponent / totals
    log_total = precision_highest + jnp.log(totals)
    mixed = jnp.einsum(
        "kuo,okq->ukq",
        attention_probs.astype(jnp.bfloat16),
        value_vectors,
        preferred_element_type=jnp.float32,
    )
    return (mixed.astype(jnp.bfloat16), log_total)


def attend_back(item):
    query_vectors, key_vectors, value_vectors, length, log_total, gradient_context_rows = item
    scores, score_scale = masked_scores(query_vectors, key_vectors, length)
    attention_probs = jnp.exp(scores - log_total)
    attention_probs_reduced = attention_probs.astype(jnp.bfloat16)
    grad_attention = jnp.einsum(
        "gyx,uyx->ygu", gradient_context_rows, value_vectors, preferred_element_type=jnp.float32
    )
    weighted = jnp.sum(attention_probs * grad_attention, axis=-1, keepdims=True)
    gradient_score_matrix = (attention_probs * (grad_attention - weighted)).astype(jnp.bfloat16)
    grad_query = (
        jnp.einsum(
            "kuo,okq->ukq", gradient_score_matrix, key_vectors, preferred_element_type=jnp.float32
        )
        * score_scale
    )
    grad_keys = (
        jnp.einsum(
            "ygu,gyp->uyp", gradient_score_matrix, query_vectors, preferred_element_type=jnp.float32
        )
        * score_scale
    )
    grad_values = jnp.einsum(
        "ygu,gyp->uyp",
        attention_probs_reduced,
        gradient_context_rows,
        preferred_element_type=jnp.float32,
    )
    return (
        grad_query.astype(jnp.bfloat16),
        grad_keys.astype(jnp.bfloat16),
        grad_values.astype(jnp.bfloat16),
    )


def shards(
    hidden_in,
    lengths,
    query_w,
    key_w,
    value_w,
    out_w,
    query_b,
    value_b,
    out_b,
    gain_one,
    shift_one,
    up_w,
    up_b,
    down_w,
    down_b,
    gain_two,
    shift_two,
    cotangent,
):
    seq_count, seq_len, width = hidden_in.shape
    token_rows = seq_count * seq_len
    heads_shape = (seq_count, seq_len, HEADS, width // HEADS)
    rows_in = hidden_in.reshape(token_rows, width)
    attn_full = (
        lax.all_gather(query_w, "fsdp", axis=0, tiled=True),
        lax.all_gather(key_w, "fsdp", axis=0, tiled=True),
        lax.all_gather(value_w, "fsdp", axis=0, tiled=True),
        lax.all_gather(out_w, "fsdp", axis=0, tiled=True),
        lax.all_gather(query_b, "fsdp", axis=0, tiled=True),
        lax.all_gather(value_b, "fsdp", axis=0, tiled=True),
        lax.all_gather(out_b, "fsdp", axis=0, tiled=True),
        lax.all_gather(gain_one, "fsdp", axis=0, tiled=True),
        lax.all_gather(shift_one, "fsdp", axis=0, tiled=True),
    )
    (
        full_query,
        full_key,
        full_value,
        full_out,
        full_query_b,
        full_value_b,
        full_out_b,
        full_gain_one,
        full_shift_one,
    ) = attn_full
    query_vectors = (
        (product(rows_in, full_query) + full_query_b).astype(jnp.bfloat16).reshape(heads_shape)
    )
    key_vectors = product(rows_in, full_key).astype(jnp.bfloat16).reshape(heads_shape)
    value_vectors = (
        (product(rows_in, full_value) + full_value_b).astype(jnp.bfloat16).reshape(heads_shape)
    )
    mixed, log_total = lax.map(attend_one, (query_vectors, key_vectors, value_vectors, lengths))
    mixed_flat = mixed.reshape(token_rows, width)
    branch = product(mixed_flat, full_out) + full_out_b
    normed_one, inverse_one = normalize(rows_in.astype(jnp.float32) + branch)
    first = normed_one * full_gain_one + full_shift_one
    first_low = first.astype(jnp.bfloat16)
    mlp_full = (
        lax.all_gather(up_w, "fsdp", axis=0, tiled=True),
        lax.all_gather(up_b, "fsdp", axis=0, tiled=True),
        lax.all_gather(down_w, "fsdp", axis=0, tiled=True),
        lax.all_gather(down_b, "fsdp", axis=0, tiled=True),
        lax.all_gather(gain_two, "fsdp", axis=0, tiled=True),
        lax.all_gather(shift_two, "fsdp", axis=0, tiled=True),
    )
    full_up, full_up_b, full_down, full_down_b, full_gain_two, full_shift_two = mlp_full
    inner = product(first_low, full_up) + full_up_b
    hidden_low = jax.nn.gelu(inner, approximate=False).astype(jnp.bfloat16)
    second = product(hidden_low, full_down) + full_down_b
    normed_two, inverse_two = normalize(first + second)
    block_out = (
        (normed_two * full_gain_two + full_shift_two).astype(jnp.bfloat16).reshape(hidden_in.shape)
    )
    positions = jnp.arange(seq_len, dtype=jnp.int32)
    valid = (positions[None, :] < lengths[:, None]).astype(jnp.float32).reshape(token_rows, 1)
    grad_top = cotangent.reshape(token_rows, width).astype(jnp.float32) * valid
    back_up, back_up_b, back_down, back_down_b, back_gain_two, back_shift_two = (
        lax.all_gather(up_w, "fsdp", axis=0, tiled=True),
        lax.all_gather(up_b, "fsdp", axis=0, tiled=True),
        lax.all_gather(down_w, "fsdp", axis=0, tiled=True),
        lax.all_gather(down_b, "fsdp", axis=0, tiled=True),
        lax.all_gather(gain_two, "fsdp", axis=0, tiled=True),
        lax.all_gather(shift_two, "fsdp", axis=0, tiled=True),
    )
    grad_gain_two = jnp.sum(grad_top * normed_two, axis=0)
    grad_shift_two = jnp.sum(grad_top, axis=0)
    grad_sum_two = norm_back(grad_top * back_gain_two, normed_two, inverse_two)
    grad_second = grad_sum_two.astype(jnp.bfloat16)
    grad_down_w = trans_left(hidden_low, grad_second)
    grad_down_b = jnp.sum(grad_second.astype(jnp.float32), axis=0)
    grad_hidden = trans_right(grad_second, back_down)
    gelu_out, gelu_pull = jax.vjp(lambda value_in: jax.nn.gelu(value_in, approximate=False), inner)
    grad_inner = gelu_pull(grad_hidden)[0].astype(jnp.bfloat16)
    grad_up_w = trans_left(first_low, grad_inner)
    grad_up_b = jnp.sum(grad_inner.astype(jnp.float32), axis=0)
    grad_first = grad_sum_two + trans_right(grad_inner, back_up)
    own_up_w, own_up_b, own_down_w, own_down_b, own_gain_two, own_shift_two = (
        lax.psum_scatter(grad_up_w, "fsdp", scatter_dimension=0, tiled=True),
        lax.psum_scatter(grad_up_b, "fsdp", scatter_dimension=0, tiled=True),
        lax.psum_scatter(grad_down_w, "fsdp", scatter_dimension=0, tiled=True),
        lax.psum_scatter(grad_down_b, "fsdp", scatter_dimension=0, tiled=True),
        lax.psum_scatter(grad_gain_two, "fsdp", scatter_dimension=0, tiled=True),
        lax.psum_scatter(grad_shift_two, "fsdp", scatter_dimension=0, tiled=True),
    )
    (
        back_query,
        back_key,
        back_value,
        back_out,
        back_query_b,
        back_value_b,
        back_out_b,
        back_gain_one,
        back_shift_one,
    ) = (
        lax.all_gather(query_w, "fsdp", axis=0, tiled=True),
        lax.all_gather(key_w, "fsdp", axis=0, tiled=True),
        lax.all_gather(value_w, "fsdp", axis=0, tiled=True),
        lax.all_gather(out_w, "fsdp", axis=0, tiled=True),
        lax.all_gather(query_b, "fsdp", axis=0, tiled=True),
        lax.all_gather(value_b, "fsdp", axis=0, tiled=True),
        lax.all_gather(out_b, "fsdp", axis=0, tiled=True),
        lax.all_gather(gain_one, "fsdp", axis=0, tiled=True),
        lax.all_gather(shift_one, "fsdp", axis=0, tiled=True),
    )
    grad_gain_one = jnp.sum(grad_first * normed_one, axis=0)
    grad_shift_one = jnp.sum(grad_first, axis=0)
    grad_sum_one = norm_back(grad_first * back_gain_one, normed_one, inverse_one)
    grad_branch = grad_sum_one.astype(jnp.bfloat16)
    grad_out_w = trans_left(mixed_flat, grad_branch)
    grad_out_b = jnp.sum(grad_branch.astype(jnp.float32), axis=0)
    gradient_context_rows = (
        trans_right(grad_branch, back_out).astype(jnp.bfloat16).reshape(heads_shape)
    )
    grad_query, grad_keys, grad_values = lax.map(
        attend_back,
        (query_vectors, key_vectors, value_vectors, lengths, log_total, gradient_context_rows),
    )
    grad_query = grad_query.reshape(token_rows, width)
    grad_keys = grad_keys.reshape(token_rows, width)
    grad_values = grad_values.reshape(token_rows, width)
    grad_query_w = trans_left(rows_in, grad_query)
    grad_query_b = jnp.sum(grad_query.astype(jnp.float32), axis=0)
    grad_key_w = trans_left(rows_in, grad_keys)
    grad_value_w = trans_left(rows_in, grad_values)
    grad_value_b = jnp.sum(grad_values.astype(jnp.float32), axis=0)
    grad_in = (
        grad_sum_one
        + trans_right(grad_query, back_query)
        + trans_right(grad_keys, back_key)
        + trans_right(grad_values, back_value)
    )
    (
        own_query_w,
        own_key_w,
        own_value_w,
        own_out_w,
        own_query_b,
        own_value_b,
        own_out_b,
        own_gain_one,
        own_shift_one,
    ) = (
        lax.psum_scatter(grad_query_w, "fsdp", scatter_dimension=0, tiled=True),
        lax.psum_scatter(grad_key_w, "fsdp", scatter_dimension=0, tiled=True),
        lax.psum_scatter(grad_value_w, "fsdp", scatter_dimension=0, tiled=True),
        lax.psum_scatter(grad_out_w, "fsdp", scatter_dimension=0, tiled=True),
        lax.psum_scatter(grad_query_b, "fsdp", scatter_dimension=0, tiled=True),
        lax.psum_scatter(grad_value_b, "fsdp", scatter_dimension=0, tiled=True),
        lax.psum_scatter(grad_out_b, "fsdp", scatter_dimension=0, tiled=True),
        lax.psum_scatter(grad_gain_one, "fsdp", scatter_dimension=0, tiled=True),
        lax.psum_scatter(grad_shift_one, "fsdp", scatter_dimension=0, tiled=True),
    )
    (
        own_query_w,
        own_key_w,
        own_value_w,
        own_out_w,
        own_query_b,
        own_value_b,
        own_out_b,
        own_gain_one,
        own_shift_one,
        own_up_w,
        own_up_b,
        own_down_w,
        own_down_b,
        own_gain_two,
        own_shift_two,
    ) = lax.psum(
        (
            own_query_w,
            own_key_w,
            own_value_w,
            own_out_w,
            own_query_b,
            own_value_b,
            own_out_b,
            own_gain_one,
            own_shift_one,
            own_up_w,
            own_up_b,
            own_down_w,
            own_down_b,
            own_gain_two,
            own_shift_two,
        ),
        "dp",
    )
    return (
        block_out,
        grad_in.reshape(hidden_in.shape),
        own_query_w,
        own_key_w,
        own_value_w,
        own_out_w,
        own_query_b,
        own_value_b,
        own_out_b,
        own_gain_one,
        own_shift_one,
        own_up_w,
        own_up_b,
        own_down_w,
        own_down_b,
        own_gain_two,
        own_shift_two,
    )


def solution(mesh):
    in_specs = (
        P(("fsdp", "dp"), None, None),
        P(("fsdp", "dp")),
        P("fsdp", None),
        P("fsdp", None),
        P("fsdp", None),
        P("fsdp", None),
        P("fsdp"),
        P("fsdp"),
        P("fsdp"),
        P("fsdp"),
        P("fsdp"),
        P("fsdp", None),
        P("fsdp"),
        P("fsdp", None),
        P("fsdp"),
        P("fsdp"),
        P("fsdp"),
        P(("fsdp", "dp"), None, None),
    )
    out_specs = (
        P(("fsdp", "dp"), None, None),
        P(("fsdp", "dp"), None, None),
        P("fsdp", None),
        P("fsdp", None),
        P("fsdp", None),
        P("fsdp", None),
        P("fsdp"),
        P("fsdp"),
        P("fsdp"),
        P("fsdp"),
        P("fsdp"),
        P("fsdp", None),
        P("fsdp"),
        P("fsdp", None),
        P("fsdp"),
        P("fsdp"),
        P("fsdp"),
    )
    return jax.shard_map(shards, mesh=mesh, in_specs=in_specs, out_specs=out_specs, check_vma=False)
```

profile of v0, /device:TPU:0, one launch (start us, length us, event | category | flops | bytes accessed | tf_op | source)
XLA Modules:
  0.0 980.0 jit_solution(10212326208908463959)
XLA Ops:
  11.3 5.2 all-gather.1
  67.4 16.6 %all-gather.20.cloned.1.call-done = bf16[768,768]{1,0:T(8,128)(2,1)} async-done(((bf16[384,768]{1,0:T(8,128)(2,1)}), bf16[768,768]{1,0:T(8,128)(2,1)}) %all-gather.20.cloned.1.call-update) | async-done | bytes 1179664 | tf_op jit(solution)/shard_map/all_gather | solution.py:132
  95.4 23.1 %while.26 = (s32[]{:T(128)}, bf16[2,512,12,64]{1,3,2,0:T(8,128)(2,1)}, f32[2,12,512,1]{2,1,3,0:T(8,128)S(1)}, bf16[2,512,12,64]{1,3,2,0:T(8,128)(2,1)}, s32[2]{0...) while((s32[]{:T(128)}, ...), condition=%wide.region_3.4_spmd, body=%wide.region_0.3_spmd.sunk | while | flops 843442688 | bytes 47427724 | solution.py:159
  128.8 43.5 %all-gather.24.cloned.1.call-done = bf16[768,3072]{1,0:T(8,128)(2,1)} async-done(((bf16[384,3072]{1,0:T(8,128)(2,1)}), bf16[768,3072]{1,0:T(8,128)(2,1)}) %all-gather.24.cloned.1.call-update) | async-done | bytes 4718608 | tf_op jit(solution)/shard_map/all_gather | solution.py:166
  172.3 35.8 %multiply_convert_fusion.3 = (bf16[1024,3072]{1,0:T(8,128)(2,1)}, f32[1024,3072]{1,0:T(8,128)}, f32[1024,3072]{1,0:T(8,128)}) fusion(f32[3072]{0:T(1024)S(1)} %bitcast.212, bf16[768,3072]{1,0:T(8,128)(2,1)} %all-gather.24.cloned.1.call-done, f32[1024,768]{1,0:T(8,128)S(1)} %get-tuple-element.296, f32[768]{0:T(1024)S(1)} %reshape.227, ...), kind=kOutput, calls=%fused_computation.66 | convolution fusion | flops 5043388416 | bytes 39348224 | tf_op jit(solution)/shard_map/dot_general | solution.py:16
  208.1 28.3 %all-gather.26.cloned.1.call-done = bf16[3072,768]{1,0:T(8,128)(2,1)} async-done(((bf16[1536,768]{1,0:T(8,128)(2,1)}), bf16[3072,768]{1,0:T(8,128)(2,1)}) %all-gather.26.cloned.1.call-update) | async-done | bytes 4718608 | tf_op jit(solution)/shard_map/all_gather | solution.py:168
  236.4 8.8 fusion.79
  252.4 19.4 %convert_reduce_fusion = (f32[3072]{0:T(1024)}, bf16[1024,3072]{1,0:T(8,128)(2,1)}) fusion(f32[1024,3072]{1,0:T(8,128)} %get-tuple-element.287, bf16[3072,768]{1,0:T(8,128)(2,1)} %all-gather.26.cloned.1.call-done, f32[1024,768]{1,0:T(8,128)} %get-tuple-element.283, f32[1024,3072]{1,0:T(8,128)} %get-tuple-element.297, f32[3072]{0:T(1024)S(1)} %bitcast.213), kind=kOutput, calls=%fused_computation.64 | convolution fusion | flops 4886098944 | bytes 39346176 | tf_op jit(solution)/shard_map/dot_general | solution.py:26
  271.9 10.6 %multiply_reduce_fusion.2 = (f32[768]{0:T(1024)}, f32[1024]{0:T(1024)S(1)}, f32[1024]{0:T(1024)S(1)}, f32[768]{0:T(1024)}, f32[1024,768]{1,0:T(8,128)S(1)}) fusion(f32[1024,768]{1,0:T(8,128)S(1)} %get-tuple-element.296, f32[1024]{0:T(1024)S(1)} %add_rsqrt_fusion.1, f32[1024]{0:T(1024)S(1)} %broadcast_multiply_fusion.4, f32[768]{0:T(1024)S(1)} %reshape.226, ...), kind=kOutput, calls=%fused_computation.83 | convolution fusion | flops 4839698432 | bytes 20472832 | tf_op jit(solution)/shard_map/dot_general | solution.py:26
  299.5 51.0 %while.27 = (s32[]{:T(128)}, bf16[2,512,12,64]{1,3,2,0:T(8,128)(2,1)}, bf16[2,512,12,64]{1,3,2,0:T(8,128)(2,1)}, bf16[2,512,12,64]{1,3,2,0:T(8,128)(2,1)}, bf16[...) while((s32[]{:T(128)}, ...), condition=%wide.region_14.15_spmd, body=%wide.region_12.14_spmd.sunk | while | flops 2062412288 | bytes 152763792 | solution.py:242
  306.5 7.3 multiply_reduce_fusion.10
  313.8 7.3 multiply_convert_fusion.5
  331.7 7.3 multiply_reduce_fusion.10
  338.9 7.2 multiply_convert_fusion.5
  370.8 10.7 %fusion.73 = f32[768,3072]{1,0:T(8,128)} fusion(bf16[1024,3072]{1,0:T(8,128)(2,1)} %get-tuple-element.302, f32[1024,768]{1,0:T(8,128)S(1)} %copy-done.5, f32[768]{0:T(1024)S(1)} %copy-done.43, f32[768]{0:T(1024)S(1)} %copy-done.41, f32[1024]{0:T(1024)S(1)} %copy-done.39, f32[1024]{0:T(1024)S(1)} %copy-done.37), kind=kOutput, calls=%fused_computation.138 | convolution fusion | flops 4835770368 | bytes 18888704 | tf_op jit(solution)/shard_map/dot_general | solution.py:20
  383.4 10.2 %fusion.69 = f32[3072,768]{1,0:T(8,128)} fusion(bf16[1024,3072]{1,0:T(8,128)(2,1)} %get-tuple-element.286, f32[1024,768]{1,0:T(8,128)S(1)} %copy-done.25), kind=kOutput, calls=%fused_computation.134 | convolution fusion | flops 4832624640 | bytes 18874368 | tf_op jit(solution)/shard_map/dot_general | solution.py:20
  393.7 36.4 %reduce-scatter.11.cloned.1.call-done = f32[384,768]{0,1:T(8,128)} async-done(((f32[768,768]{0,1:T(8,128)}), f32[384,768]{0,1:T(8,128)}) %reduce-scatter.11.cloned.1.call-update) | async-done | bytes 1179664 | tf_op jit(solution)/shard_map/reduce_scatter | solution.py:273
  430.1 36.9 %reduce-scatter.9.cloned.1.call-done = f32[384,768]{0,1:T(8,128)} async-done(((f32[768,768]{0,1:T(8,128)}), f32[384,768]{0,1:T(8,128)}) %reduce-scatter.9.cloned.1.call-update) | async-done | bytes 1179664 | tf_op jit(solution)/shard_map/reduce_scatter | solution.py:272
  467.0 112.9 %reduce-scatter.15.cloned.1.call-done = f32[384,3072]{1,0:T(8,128)} async-done(((f32[768,3072]{1,0:T(8,128)}), f32[384,3072]{1,0:T(8,128)}) %reduce-scatter.15.cloned.1.call-update) | async-done | bytes 4718608 | tf_op jit(solution)/shard_map/reduce_scatter | solution.py:205
  579.9 112.8 %reduce-scatter.17.cloned.1.call-done = f32[1536,768]{1,0:T(8,128)} async-done(((f32[3072,768]{1,0:T(8,128)}), f32[1536,768]{1,0:T(8,128)}) %reduce-scatter.17.cloned.1.call-update) | async-done | bytes 4718608 | tf_op jit(solution)/shard_map/reduce_scatter | solution.py:207
  695.9 7.6 all-reduce.11
  704.2 62.9 %all-reduce.9 = (f32[384]{0:T(512)}, f32[384]{0:T(512)}, f32[384]{0:T(512)}, f32[384]{0:T(512)}, f32[384]{0:T(512)}, /*index=5*/f32[1536]{0:T(1024)}, f32[384]{0:T(512)}, f32[384]{0:T(512)}, f32[384]{0:T(512)}) all-reduce(f32[384]{0:T(512)S(1)} %dynamic-slice.1, f32[384]{0:T(512)S(1)} %dynamic-slice.3, ...), channel_id=1, replica_groups=mesh['fsdp'=2,'dp'=16] {'dp'}, use_global_device_ids=true, to_apply=%region_25.26 | all-reduce | flops 4608 | bytes 36864 | tf_op jit(solution)/shard_map/psum | solution.py:297
  776.5 182.2 %all-reduce.14.cloned.1.call-done = (f32[384,768]{0,1:T(8,128)}, f32[384,768]{0,1:T(8,128)}, f32[384,768]{0,1:T(8,128)}, f32[384,768]{1,0:T(8,128)}, f32[384,3072]{1,0:T(8,128)}, /*index=5*/f32[1536,768]{1,0:T(8,128)}) async-done(((f32[384,768]{0,1:T(8,128)}, f32[384,768]{0,1:T(8,128)}, f32[384,768]{0,1:T(8,128)}, f32[384,768]{1,0:T(8,128)}, f32[384,3072]{1,0:T(8,128)}, /*index=5*/f32[1536,768]{1,0:T(8,128)}), ...) | async-done | bytes 14155792 | tf_op jit(solution)/shard_map/psum | solution.py:297
  965.4 5.7 copy.138
  (334 shorter events, 186.8 us)
Async XLA Ops:
  7.2 48.4 %all-gather.16.cloned.1.call-start = ((), (), s32[]{:S(2)}) async-start(), calls=%async_computation.6 | async-start | bytes 1769472 | tf_op jit(solution)/shard_map/all_gather | solution.py:133
  8.0 54.2 %all-gather.18.cloned.1.call-start = ((), (), s32[]{:S(2)}) async-start(), calls=%async_computation.7 | async-start | bytes 1769472 | tf_op jit(solution)/shard_map/all_gather | solution.py:131
  8.7 30.4 %copy-start.64 = (bf16[384]{0:T(512)(128)(2,1)S(1)}, bf16[384]{0:T(512)(128)(2,1)}, u32[]{:S(2)}) copy-start(bf16[384]{0:T(512)(128)(2,1)} %param.37) | copy-start | bytes 2308
  8.7 34.8 %copy-start.65 = (bf16[384]{0:T(512)(128)(2,1)S(1)}, bf16[384]{0:T(512)(128)(2,1)}, u32[]{:S(2)}) copy-start(bf16[384]{0:T(512)(128)(2,1)} %param.38) | copy-start | bytes 2308
  8.8 39.8 %copy-start.55 = (bf16[1536]{0:T(1024)(128)(2,1)S(1)}, bf16[1536]{0:T(1024)(128)(2,1)}, u32[]{:S(2)}) copy-start(bf16[1536]{0:T(1024)(128)(2,1)} %param.34) | copy-start | bytes 9220
  8.8 44.3 %copy-start.66 = (s32[2]{0:T(128)S(1)}, s32[2]{0:T(128)}, u32[]{:S(2)}) copy-start(s32[2]{0:T(128)} %param.23) | copy-start | bytes 28
  8.8 44.9 %copy-start.9 = (bf16[2,512,768]{2,1,0:T(8,128)(2,1)S(1)}, bf16[2,512,768]{2,1,0:T(8,128)(2,1)}, u32[]{:S(2)}) copy-start(bf16[2,512,768]{2,1,0:T(8,128)(2,1)} %param.39) | copy-start | bytes 4718596
  8.8 75.2 %all-gather.20.cloned.1.call-start = ((), (), s32[]{:S(2)}) async-start(), calls=%async_computation.8 | async-start | bytes 1769472 | tf_op jit(solution)/shard_map/all_gather | solution.py:132
  9.5 114.9 %all-gather.22.cloned.1.call-start = ((), (), s32[]{:S(2)}) async-start(), calls=%async_computation.9 | async-start | bytes 1769472 | tf_op jit(solution)/shard_map/all_gather | solution.py:134
  10.1 162.2 %all-gather.24.cloned.1.call-start = ((), (), s32[]{:S(2)}) async-start(), calls=%async_computation.10 | async-start | bytes 7077888 | tf_op jit(solution)/shard_map/all_gather | solution.py:166
  10.7 225.7 %all-gather.26.cloned.1.call-start = ((), (), s32[]{:S(2)}) async-start(), calls=%async_computation.11 | async-start | bytes 7077888 | tf_op jit(solution)/shard_map/all_gather | solution.py:168
  11.3 382.4 %reduce-scatter.13.cloned.1.call-start = ((), (), s32[]{:S(2)}) async-start(), calls=%async_computation.15 | async-start | bytes 3538944 | tf_op jit(solution)/shard_map/reduce_scatter | solution.py:274
  29.8 252.6 %copy-start.40 = (f32[768]{0:T(1024)}, f32[768]{0:T(1024)S(1)}, u32[]{:S(2)}) copy-start(f32[768]{0:T(1024)S(1)} %reshape.226) | copy-start | bytes 9220
  34.2 202.2 %copy-start.42 = (f32[768]{0:T(1024)}, f32[768]{0:T(1024)S(1)}, u32[]{:S(2)}) copy-start(f32[768]{0:T(1024)S(1)} %reshape.227) | copy-start | bytes 9220
  128.3 154.1 %copy-start.4 = (f32[1024,768]{1,0:T(8,128)}, f32[1024,768]{1,0:T(8,128)S(1)}, u32[]{:S(2)}) copy-start(f32[1024,768]{1,0:T(8,128)S(1)} %get-tuple-element.296) | copy-start | bytes 9437188
  128.3 154.1 %copy-start.36 = (f32[1024]{0:T(1024)}, f32[1024]{0:T(1024)S(1)}, u32[]{:S(2)}) copy-start(f32[1024]{0:T(1024)S(1)} %broadcast_multiply_fusion.4) | copy-start | bytes 12292
  128.8 153.6 %copy-start.38 = (f32[1024]{0:T(1024)}, f32[1024]{0:T(1024)S(1)}, u32[]{:S(2)}) copy-start(f32[1024]{0:T(1024)S(1)} %add_rsqrt_fusion.1) | copy-start | bytes 12292
  172.3 64.1 %copy-start.54 = (f32[768]{0:T(1024)S(1)}, f32[768]{0:T(1024)}, u32[]{:S(2)}) copy-start(f32[768]{0:T(1024)} %reshape.229) | copy-start | bytes 9220
  295.5 98.2 %reduce-scatter.7.cloned.1.call-start = ((), (), s32[]{:S(2)}) async-start(), calls=%async_computation.12 | async-start | bytes 3538944 | tf_op jit(solution)/shard_map/reduce_scatter | solution.py:271
  358.1 72.0 %reduce-scatter.11.cloned.1.call-start = ((), (), s32[]{:S(2)}) async-start(), calls=%async_computation.14 | async-start | bytes 3538944 | tf_op jit(solution)/shard_map/reduce_scatter | solution.py:273
  364.6 102.4 %reduce-scatter.9.cloned.1.call-start = ((), (), s32[]{:S(2)}) async-start(), calls=%async_computation.13 | async-start | bytes 3538944 | tf_op jit(solution)/shard_map/reduce_scatter | solution.py:272
  370.7 209.1 %reduce-scatter.15.cloned.1.call-start = ((), (), s32[]{:S(2)}) async-start(), calls=%async_computation.16 | async-start | bytes 14155776 | tf_op jit(solution)/shard_map/reduce_scatter | solution.py:205
  381.6 311.1 %reduce-scatter.17.cloned.1.call-start = ((), (), s32[]{:S(2)}) async-start(), calls=%async_computation.17 | async-start | bytes 14155776 | tf_op jit(solution)/shard_map/reduce_scatter | solution.py:207
  393.6 565.1 %all-reduce.14.cloned.1.call-start = ((), (), s32[]{:S(2)}) async-start(), calls=%async_computation.18 | async-start | bytes 28311552 | tf_op jit(solution)/shard_map/psum | solution.py:297
  (74 other events, 314.4 us)
Sparse Core Ops, SparseCore 0:
  9.6 25.5 all-gather.15
  36.7 22.8 all-gather.17
  61.2 22.7 all-gather.19
  85.4 22.7 all-gather.21
  109.6 62.6 all-gather.23
  173.7 62.6 all-gather.25
  295.6 34.7 reduce-scatter.12
  358.2 34.8 reduce-scatter.6
  395.3 34.7 reduce-scatter.10
  432.2 34.6 reduce-scatter.8
  469.3 110.5 reduce-scatter.14
  582.0 110.5 reduce-scatter.16
  697.8 260.9 all-reduce.13
where the time goes:
time: 987 us; the launch traced here: 980 us
  waiting for transfers between devices  573 us (58%)
  matrix products  177 us (18%)
  blocking collectives  111 us (11%)
  local copies, waits for them, and re-layouts  67.4 us (7%)
  other arithmetic  33 us (3%)
  between operations  16.4 us (2%)
    psum x1, waiting for transfers between devices, shards(): lax.psum((own_query_w, own_key_w, own_value_w, own_out_w, own_query_b, ow...  182 us
    reduce_scatter x1, waiting for transfers between devices, shards(): lax.psum_scatter(grad_up_w, 'fsdp', scatter_dimension=0, tiled=True)  113 us
    reduce_scatter x1, waiting for transfers between devices, shards(): lax.psum_scatter(grad_down_w, 'fsdp', scatter_dimension=0, tiled=True)  113 us
    psum x1, blocking collectives, shards(): lax.psum((own_query_w, own_key_w, own_value_w, own_out_w, own_query_b, ow...  62.9 us
    dot_general x6, matrix products, product(): return jnp.dot(left, right, preferred_element_type=jnp.float32)  58.5 us
    all_gather x1, waiting for transfers between devices, shards(): lax.all_gather(up_w, 'fsdp', axis=0, tiled=True)  43.5 us
    dot_general x6, matrix products, trans_right(): lax.dot_general(left, right, (((1,), (1,)), ((), ())), preferred_element_...  41.4 us
    reduce_scatter x1, waiting for transfers between devices, shards(): lax.psum_scatter(grad_key_w, 'fsdp', scatter_dimension=0, tiled=True)  36.9 us
  transfers between devices with their start and end apart: 13, of which 8 were waited for; matrix products, arithmetic and copies ran while one was open for 20% of the time, Pallas kernels for 0%

commit v1 on v0

v1 whole, which is shorter than its diff:
```python
import math

import jax
import jax.numpy as jnp
from jax import lax
from jax.sharding import PartitionSpec as P

HEADS = 12


norm_eps = 1e-12
mask_fill = -1e30


def product(left, right):
    return jnp.dot(left, right, preferred_element_type=jnp.float32)


def trans_left(left, right):
    return lax.dot_general(
        left, right, (((0,), (0,)), ((), ())), preferred_element_type=jnp.float32
    )


def trans_right(left, right):
    return lax.dot_general(
        left, right, (((1,), (1,)), ((), ())), preferred_element_type=jnp.float32
    )


def normalize(summed):
    average = jnp.mean(summed, axis=-1, keepdims=True)
    centred = summed - average
    inverse = lax.rsqrt(jnp.mean(centred * centred, axis=-1, keepdims=True) + norm_eps)
    return (centred * inverse, inverse)


def norm_back(grad_normed, normed, inverse):
    first_mean = jnp.mean(grad_normed, axis=-1, keepdims=True)
    cross_mean = jnp.mean(grad_normed * normed, axis=-1, keepdims=True)
    return inverse * (grad_normed - first_mean - normed * cross_mean)


def masked_scores(query_vectors, key_vectors, length):
    score_scale = 1.0 / math.sqrt(query_vectors.shape[-1])
    unmasked_score_matrix = (
        jnp.einsum("gyx,uyx->ygu", query_vectors, key_vectors, preferred_element_type=jnp.float32)
        * score_scale
    )
    allowed = jnp.arange(key_vectors.shape[0], dtype=jnp.int32) < length
    return (jnp.where(allowed[None, None, :], unmasked_score_matrix, mask_fill), score_scale)


def attend_one(item):
    query_vectors, key_vectors, value_vectors, length = item
    scores, score_scale = masked_scores(query_vectors, key_vectors, length)
    precision_highest = jnp.max(scores, axis=-1, keepdims=True)
    exponent = jnp.exp(scores - precision_highest)
    totals = jnp.sum(exponent, axis=-1, keepdims=True)
    attention_probs = exponent / totals
    log_total = precision_highest + jnp.log(totals)
    mixed = jnp.einsum(
        "kuo,okq->ukq",
        attention_probs.astype(jnp.bfloat16),
        value_vectors,
        preferred_element_type=jnp.float32,
    )
    return (mixed.astype(jnp.bfloat16), log_total)


def attend_back(item):
    query_vectors, key_vectors, value_vectors, length, log_total, gradient_context_rows = item
    scores, score_scale = masked_scores(query_vectors, key_vectors, length)
    attention_probs = jnp.exp(scores - log_total)
    attention_probs_reduced = attention_probs.astype(jnp.bfloat16)
    grad_attention = jnp.einsum(
        "gyx,uyx->ygu", gradient_context_rows, value_vectors, preferred_element_type=jnp.float32
    )
    weighted = jnp.sum(attention_probs * grad_attention, axis=-1, keepdims=True)
    gradient_score_matrix = (attention_probs * (grad_attention - weighted)).astype(jnp.bfloat16)
    grad_query = (
        jnp.einsum(
            "kuo,okq->ukq", gradient_score_matrix, key_vectors, preferred_element_type=jnp.float32
        )
        * score_scale
    )
    grad_keys = (
        jnp.einsum(
            "ygu,gyp->uyp", gradient_score_matrix, query_vectors, preferred_element_type=jnp.float32
        )
        * score_scale
    )
    grad_values = jnp.einsum(
        "ygu,gyp->uyp",
        attention_probs_reduced,
        gradient_context_rows,
        preferred_element_type=jnp.float32,
    )
    return (
        grad_query.astype(jnp.bfloat16),
        grad_keys.astype(jnp.bfloat16),
        grad_values.astype(jnp.bfloat16),
    )


def core_pairs():
    count = lax.axis_size("dp")
    return [(index, index ^ 1) for index in range(count)]


def same_core_groups():
    count = lax.axis_size("dp")
    return [list(range(core, count, 2)) for core in range(2)]


def own_core():
    return lax.rem(lax.axis_index("dp"), 2)


def join_cores(mine, theirs):
    lower = own_core() == 0
    return jnp.stack([jnp.where(lower, mine, theirs), jnp.where(lower, theirs, mine)], axis=-3)


def gather_weight(shard):
    rows, columns = shard.shape
    half = rows // 2
    mine = lax.dynamic_slice_in_dim(shard, own_core() * half, half, axis=0)
    mine = lax.all_gather(mine, "fsdp", axis=0, tiled=False)
    theirs = lax.ppermute(mine, "dp", core_pairs())
    return join_cores(mine, theirs).reshape(-1, columns)


def gather_vectors(vectors):
    whole = lax.all_gather(jnp.concatenate(vectors), "fsdp", axis=0, tiled=False)
    pieces, start = [], 0
    for vector in vectors:
        size = vector.shape[0]
        pieces.append(whole[:, start : start + size].reshape(-1).astype(jnp.float32))
        start += size
    return pieces


def core_sum(grad):
    groups = lax.axis_size("fsdp")
    rows, columns = grad.shape
    cut = grad.astype(jnp.bfloat16).reshape(groups, 2, rows // (2 * groups), columns)
    core = own_core()
    kept = lax.dynamic_index_in_dim(cut, core, axis=1, keepdims=False)
    sent = lax.dynamic_index_in_dim(cut, 1 - core, axis=1, keepdims=False)
    return (
        kept.astype(jnp.float32) + lax.ppermute(sent, "dp", core_pairs()).astype(jnp.float32)
    ).astype(jnp.bfloat16)


def scatter_weight(grad):
    return lax.psum_scatter(core_sum(grad), "fsdp", scatter_dimension=0, tiled=False)


def sum_replicas(parts):
    return lax.psum(parts, "dp", axis_index_groups=same_core_groups())


def both_cores(part):
    theirs = lax.ppermute(part, "dp", core_pairs())
    return join_cores(part, theirs).reshape(-1, part.shape[-1]).astype(jnp.float32)


def sum_vectors(grads):
    groups = lax.axis_size("fsdp")
    packed = jnp.concatenate([grad.reshape(groups, -1) for grad in grads], axis=1)
    packed = lax.psum(packed, ("fsdp", "dp"))
    mine = lax.dynamic_index_in_dim(packed, lax.axis_index("fsdp"), axis=0, keepdims=False)
    pieces, start = [], 0
    for grad in grads:
        size = grad.shape[0] // groups
        pieces.append(mine[start : start + size])
        start += size
    return pieces


def gelu_pair(inner):
    bell = jnp.exp(-0.5 * inner * inner)
    size = jnp.abs(inner) * (1.0 / math.sqrt(2.0))
    step = 1.0 / (1.0 + 0.3275911 * size)
    poly = step * (
        0.254829592
        + step * (-0.284496736 + step * (1.421413741 + step * (-1.453152027 + step * 1.061405429)))
    )
    tail = 0.5 * poly * bell
    share = jnp.where(inner < 0, tail, 1.0 - tail)
    slope = share + inner * bell * (1.0 / math.sqrt(2.0 * math.pi))
    return (inner * share).astype(jnp.bfloat16), slope.astype(jnp.bfloat16)


def shards(
    hidden_in,
    lengths,
    query_w,
    key_w,
    value_w,
    out_w,
    query_b,
    value_b,
    out_b,
    gain_one,
    shift_one,
    up_w,
    up_b,
    down_w,
    down_b,
    gain_two,
    shift_two,
    cotangent,
):
    seq_count, seq_len, width = hidden_in.shape
    token_rows = seq_count * seq_len
    heads_shape = (seq_count, seq_len, HEADS, width // HEADS)
    rows_in = hidden_in.reshape(token_rows, width)
    full_qkv = gather_weight(jnp.concatenate([query_w, key_w, value_w], axis=1))
    (
        full_query_b,
        full_value_b,
        full_out_b,
        full_gain_one,
        full_shift_one,
        full_up_b,
        full_down_b,
        full_gain_two,
        full_shift_two,
    ) = gather_vectors(
        [query_b, value_b, out_b, gain_one, shift_one, up_b, down_b, gain_two, shift_two]
    )
    full_out = gather_weight(out_w)
    full_up = gather_weight(up_w)
    full_down = gather_weight(down_w)
    qkv_bias = jnp.concatenate([full_query_b, jnp.zeros_like(full_query_b), full_value_b])
    qkv = (product(rows_in, full_qkv) + qkv_bias).astype(jnp.bfloat16)
    query_vectors, key_vectors, value_vectors = (
        part.reshape(heads_shape) for part in jnp.split(qkv, 3, axis=1)
    )
    mixed, log_total = lax.map(attend_one, (query_vectors, key_vectors, value_vectors, lengths))
    mixed_flat = mixed.reshape(token_rows, width)
    branch = product(mixed_flat, full_out) + full_out_b
    normed_one, inverse_one = normalize(rows_in.astype(jnp.float32) + branch)
    first = normed_one * full_gain_one + full_shift_one
    first_low = first.astype(jnp.bfloat16)
    inner = product(first_low, full_up) + full_up_b
    hidden_low, slope_low = gelu_pair(inner)
    second = product(hidden_low, full_down) + full_down_b
    normed_two, inverse_two = normalize(first + second)
    block_out = (
        (normed_two * full_gain_two + full_shift_two).astype(jnp.bfloat16).reshape(hidden_in.shape)
    )
    positions = jnp.arange(seq_len, dtype=jnp.int32)
    valid = (positions[None, :] < lengths[:, None]).astype(jnp.float32).reshape(token_rows, 1)
    grad_top = cotangent.reshape(token_rows, width).astype(jnp.float32) * valid
    grad_gain_two = jnp.sum(grad_top * normed_two, axis=0)
    grad_shift_two = jnp.sum(grad_top, axis=0)
    grad_sum_two = norm_back(grad_top * full_gain_two, normed_two, inverse_two)
    grad_second = grad_sum_two.astype(jnp.bfloat16)
    part_down = scatter_weight(trans_left(hidden_low, grad_second))
    grad_down_b = jnp.sum(grad_second.astype(jnp.float32), axis=0)
    grad_hidden = trans_right(grad_second, full_down)
    grad_inner = (grad_hidden * slope_low.astype(jnp.float32)).astype(jnp.bfloat16)
    part_up = scatter_weight(trans_left(first_low, grad_inner))
    grad_up_b = jnp.sum(grad_inner.astype(jnp.float32), axis=0)
    part_up, part_down = sum_replicas((part_up, part_down))
    grad_first = grad_sum_two + trans_right(grad_inner, full_up)
    grad_gain_one = jnp.sum(grad_first * normed_one, axis=0)
    grad_shift_one = jnp.sum(grad_first, axis=0)
    grad_sum_one = norm_back(grad_first * full_gain_one, normed_one, inverse_one)
    grad_branch = grad_sum_one.astype(jnp.bfloat16)
    part_out = scatter_weight(trans_left(mixed_flat, grad_branch))
    grad_out_b = jnp.sum(grad_branch.astype(jnp.float32), axis=0)
    grad_mixed = trans_right(grad_branch, full_out).astype(jnp.bfloat16)
    grad_query, grad_keys, grad_values = lax.map(
        attend_back,
        (
            query_vectors,
            key_vectors,
            value_vectors,
            lengths,
            log_total,
            grad_mixed.reshape(heads_shape),
        ),
    )
    grad_qkv = jnp.concatenate(
        [part.reshape(token_rows, width) for part in (grad_query, grad_keys, grad_values)], axis=1
    )
    grad_qkv_b = jnp.sum(grad_qkv.astype(jnp.float32), axis=0)
    part_qkv = scatter_weight(trans_left(rows_in, grad_qkv))
    grad_in = grad_sum_one + trans_right(grad_qkv, full_qkv)
    (
        own_query_b,
        own_value_b,
        own_out_b,
        own_gain_one,
        own_shift_one,
        own_up_b,
        own_down_b,
        own_gain_two,
        own_shift_two,
    ) = sum_vectors(
        [
            grad_qkv_b[:width],
            grad_qkv_b[2 * width :],
            grad_out_b,
            grad_gain_one,
            grad_shift_one,
            grad_up_b,
            grad_down_b,
            grad_gain_two,
            grad_shift_two,
        ]
    )
    part_out, part_qkv, part_up, part_down = lax.optimization_barrier(
        (part_out, part_qkv, part_up, part_down)
    )
    part_out, part_qkv = sum_replicas((part_out, part_qkv))
    own_up_w, own_down_w, own_out_w, own_qkv_w = (
        both_cores(part) for part in (part_up, part_down, part_out, part_qkv)
    )
    own_query_w, own_key_w, own_value_w = jnp.split(own_qkv_w, 3, axis=1)
    return (
        block_out,
        grad_in.reshape(hidden_in.shape),
        own_query_w,
        own_key_w,
        own_value_w,
        own_out_w,
        own_query_b,
        own_value_b,
        own_out_b,
        own_gain_one,
        own_shift_one,
        own_up_w,
        own_up_b,
        own_down_w,
        own_down_b,
        own_gain_two,
        own_shift_two,
    )


def solution(mesh):
    in_specs = (
        P(("fsdp", "dp"), None, None),
        P(("fsdp", "dp")),
        P("fsdp", None),
        P("fsdp", None),
        P("fsdp", None),
        P("fsdp", None),
        P("fsdp"),
        P("fsdp"),
        P("fsdp"),
        P("fsdp"),
        P("fsdp"),
        P("fsdp", None),
        P("fsdp"),
        P("fsdp", None),
        P("fsdp"),
        P("fsdp"),
        P("fsdp"),
        P(("fsdp", "dp"), None, None),
    )
    out_specs = (
        P(("fsdp", "dp"), None, None),
        P(("fsdp", "dp"), None, None),
        P("fsdp", None),
        P("fsdp", None),
        P("fsdp", None),
        P("fsdp", None),
        P("fsdp"),
        P("fsdp"),
        P("fsdp"),
        P("fsdp"),
        P("fsdp"),
        P("fsdp", None),
        P("fsdp"),
        P("fsdp", None),
        P("fsdp"),
        P("fsdp"),
        P("fsdp"),
    )
    return jax.shard_map(shards, mesh=mesh, in_specs=in_specs, out_specs=out_specs, check_vma=False)
```

time: 987 us -> 643 us (0.65)
  waiting for transfers between devices: 573 us -> 267 us
  blocking collectives: 111 us -> 59.6 us
  matrix products: 177 us -> 143 us
  other arithmetic: 33 us -> 65.2 us
  local copies, waits for them, and re-layouts: 67.4 us -> 80.4 us
    reduce_scatter x6 -> x4, waiting for transfers between devices: 299 us -> 38.4 us  [scatter_weight(): lax.psum_scatter(core_sum(grad), 'fsdp', scatter_dimension=0, tiled=False)]
    psum x1 -> x2, waiting for transfers between devices: 182 us -> 144 us  [sum_replicas(): return lax.psum(parts, 'dp', axis_index_groups=same_core_groups())]
    dot_general x6 -> x4, matrix products: 58.5 us -> 31.5 us  [product(): return jnp.dot(left, right, preferred_element_type=jnp.float32)]
    psum x1, blocking collectives: 62.9 us -> 40.9 us  [sum_vectors(): packed = lax.psum(packed, ('fsdp', 'dp'))]
    all_gather x9 -> x2, blocking collectives: 40 us -> 18.7 us  [the longest x1 13.3 us: gather_weight(): mine = lax.all_gather(mine, 'fsdp', axis=0, tiled=False)]
    convert_element_type x9 -> x10, other arithmetic: 0.18 us -> 18 us  [the longest x4 10.9 us: core_sum(): return (kept.astype(jnp.float32) + lax.ppermute(sent, 'dp', core_pairs())...]
    dot_general x6 -> x4, matrix products: 32.2 us -> 20.8 us  [trans_left(): lax.dot_general(left, right, (((0,), (0,)), ((), ())), preferred_element_...]
    unnamed x165 -> x156, local copies, waits for them, and re-layouts: 29.8 us -> 18.8 us
  transfers between devices with their start and end apart: 13 -> 21, of which waited for: 8 -> 8; matrix products, arithmetic and copies ran while one was open for 20% -> 36% of each run, Pallas kernels for 0% -> 0%
where the time goes in v1:
time: 643 us; the launch traced here: 635 us
  waiting for transfers between devices  267 us (42%)
  matrix products  143 us (22%)
  local copies, waits for them, and re-layouts  80.4 us (13%)
  other arithmetic  65.2 us (10%)
  blocking collectives  59.6 us (9%)
  between operations  15.4 us (2%)
    psum x2, waiting for transfers between devices, sum_replicas(): return lax.psum(parts, 'dp', axis_index_groups=same_core_groups())  144 us
    all_gather x3, waiting for transfers between devices, gather_weight(): mine = lax.all_gather(mine, 'fsdp', axis=0, tiled=False)  81.5 us
    psum x1, blocking collectives, sum_vectors(): packed = lax.psum(packed, ('fsdp', 'dp'))  40.9 us
    dot_general x4, matrix products, trans_right(): lax.dot_general(left, right, (((1,), (1,)), ((), ())), preferred_element_...  39.9 us
    reduce_scatter x4, waiting for transfers between devices, scatter_weight(): lax.psum_scatter(core_sum(grad), 'fsdp', scatter_dimension=0, tiled=False)  38.4 us
    dot_general x4, matrix products, product(): return jnp.dot(left, right, preferred_element_type=jnp.float32)  31.5 us
    dot_general x4, matrix products, trans_left(): lax.dot_general(left, right, (((0,), (0,)), ((), ())), preferred_element_...  20.8 us
    unnamed x156, local copies, waits for them, and re-layouts  18.8 us
  transfers between devices with their start and end apart: 21, of which 8 were waited for; matrix products, arithmetic and copies ran while one was open for 36% of the time, Pallas kernels for 0%

profile of v1, /device:TPU:0, one launch (start us, length us, event | category | flops | bytes accessed | tf_op | source)
XLA Modules:
  0.0 634.8 jit_solution(8452154974374657386)
XLA Ops:
  13.5 13.3 %all-gather.2 = bf16[384,768]{1,0:T(8,128)(2,1)S(1)} all-gather(bf16[192,768]{1,0:T(8,128)(2,1)S(1)} %constant_dynamic-slice_fusion.3), channel_id=4, replica_groups=mesh['fsdp'=2,'dp'=16] {'fsdp'}, dimensions={0}, use_global_device_ids=true | all-gather | bytes 884736 | tf_op jit(solution)/shard_map/all_gather | solution.py:129
  28.9 5.4 all-gather.5
  34.3 9.4 %all-gather.10.cloned.1.call-done = bf16[384,2304]{1,0:T(8,128)(2,1)} async-done(((bf16[192,2304]{1,0:T(8,128)(2,1)}), bf16[384,2304]{1,0:T(8,128)(2,1)}) %all-gather.10.cloned.1.call-update) | async-done | bytes 1769488 | tf_op jit(solution)/shard_map/all_gather | solution.py:129
  49.6 33.8 %all-gather.12.cloned.1.call-done = bf16[384,3072]{1,0:T(8,128)(2,1)} async-done(((bf16[192,3072]{1,0:T(8,128)(2,1)}), bf16[384,3072]{1,0:T(8,128)(2,1)}) %all-gather.12.cloned.1.call-update) | async-done | bytes 2359312 | tf_op jit(solution)/shard_map/all_gather | solution.py:129
  83.5 38.2 %all-gather.14.cloned.1.call-done = bf16[1536,768]{1,0:T(8,128)(2,1)} async-done(((bf16[768,768]{1,0:T(8,128)(2,1)}), bf16[1536,768]{1,0:T(8,128)(2,1)}) %all-gather.14.cloned.1.call-update) | async-done | bytes 2359312 | tf_op jit(solution)/shard_map/all_gather | solution.py:129
  125.6 5.0 fusion.63
  151.6 24.9 %while.26 = (s32[]{:T(128)}, bf16[2,512,12,64]{1,3,2,0:T(8,128)(2,1)}, f32[2,12,512,1]{2,1,3,0:T(8,128)S(1)}, bf16[2,512,12,64]{1,3,2,0:T(8,128)(2,1)}, s32[2]{0...) while((s32[]{:T(128)}, ...), condition=%wide.region_3.4_spmd, body=%wide.region_0.3_spmd.sunk | while | flops 843442688 | bytes 47427716 | solution.py:242
  192.2 17.3 %multiply_convert_fusion.4 = (bf16[1024,3072]{1,0:T(8,128)(2,1)}, f32[1024,3072]{1,0:T(8,128)}) fusion(f32[3072]{0:T(1024)S(1)} %copy-done.50, bf16[768,3072]{1,0:T(8,128)(2,1)S(1)} %bitcast.279, f32[1024,768]{1,0:T(8,128)S(1)} %get-tuple-element.271, f32[768]{0:T(1024)S(1)} %copy-done.54, f32[768]{0:T(1024)S(1)} %copy-done.45, ...), kind=kOutput, calls=%fused_computation.72 | convolution fusion | flops 4908122112 | bytes 26765312 | tf_op jit(solution)/shard_map/dot_general | solution.py:16
  209.5 7.5 %fusion.86 = (f32[1024]{0:T(1024)S(1)}, f32[1024,768]{1,0:T(8,128)S(1)}) fusion(f32[768]{0:T(1024)S(1)} %copy-done.55, bf16[1024,3072]{1,0:T(8,128)(2,1)} %get-tuple-element.272, bf16[3072,768]{1,0:T(8,128)(2,1)S(1)} %bitcast.283, f32[768]{0:T(1024)S(1)} %copy-done.54, f32[768]{0:T(1024)S(1)} %copy-done.45, f32[1024]{0:T(1024)S(1)} %add_rsqrt_fusion.1, ...), kind=kOutput, calls=%fused_computation.206 | convolution fusion | flops 4837342208 | bytes 17323008 | tf_op jit(solution)/shard_map/dot_general | solution.py:16
  223.8 5.7 convolution_convert_fusion
  230.2 18.5 %convert_reduce_fusion = (f32[3072]{0:T(1024)}, bf16[1024,3072]{1,0:T(8,128)(2,1)}) fusion(f32[1024,3072]{1,0:T(8,128)} %get-tuple-element.273, f32[3072]{0:T(1024)S(1)} %copy-done.50, bf16[3072,768]{1,0:T(8,128)(2,1)S(1)} %bitcast.284, f32[1024,768]{1,0:T(8,128)S(1)} %get-tuple-element.228), kind=kOutput, calls=%fused_computation.70 | convolution fusion | flops 4926993408 | bytes 26763264 | tf_op jit(solution)/shard_map/dot_general | solution.py:26
  250.9 9.6 %convolution_convert_fusion.1 = bf16[768,3072]{1,0:T(8,128)(2,1)S(1)} fusion(bf16[1024,3072]{1,0:T(8,128)(2,1)} %get-tuple-element.278, f32[1024,768]{1,0:T(8,128)} %copy-done.10, f32[768]{0:T(1024)S(1)} %copy-done.54, f32[768]{0:T(1024)S(1)} %copy-done.45, f32[1024]{0:T(1024)S(1)} %add_rsqrt_fusion.1, f32[1024]{0:T(1024)S(1)} %broadcast_multiply_fusion.4), kind=kOutput, calls=%fused_computation.76 | convolution fusion | flops 4838129664 | bytes 14170112 | tf_op jit(solution)/shard_map/dot_general | solution.py:20
  264.5 8.8 %multiply_reduce_fusion.2 = (f32[768]{0:T(1024)}, f32[1024]{0:T(1024)S(1)}, f32[1024]{0:T(1024)S(1)}, f32[768]{0:T(1024)}, f32[1024,768]{1,0:T(8,128)S(1)}) fusion(f32[1024,768]{1,0:T(8,128)S(1)} %copy-done.11, f32[1024]{0:T(1024)S(1)} %add_rsqrt_fusion.1, f32[1024]{0:T(1024)S(1)} %broadcast_multiply_fusion.4, f32[768]{0:T(1024)S(1)} %copy-done.45, ...), kind=kOutput, calls=%fused_computation.91 | convolution fusion | flops 4839698432 | bytes 20472832 | tf_op jit(solution)/shard_map/dot_general | solution.py:26
  295.0 54.7 %while.27 = (s32[]{:T(128)}, bf16[2,512,12,64]{1,3,2,0:T(8,128)(2,1)}, bf16[2,512,12,64]{1,3,2,0:T(8,128)(2,1)}, bf16[2,512,12,64]{1,3,2,0:T(8,128)(2,1)}, bf16[...) while((s32[]{:T(128)}, ...), condition=%wide.region_14.15_spmd, body=%wide.region_12.14_spmd.sunk | while | flops 2062412288 | bytes 146472272 | solution.py:277
  299.6 7.3 %multiply_reduce_fusion.10 = (f32[12,512]{1,0:T(8,128)S(1)}, f32[12,512,512]{1,2,0:T(8,128)}) fusion(f32[12,512,512]{1,2,0:T(8,128)S(1)} %fusion.135, f32[12,512]{1,0:T(8,128)S(1)} %dynamic-slice_bitcast_fusion.6, pred[512]{0:T(512)(128)(4,1)S(1)} %iota_compare_fusion.5, bf16[2,512,12,64]{1,3,2,0:T(8,128)(2,1)S(1)} %copy-done.6, ...), kind=kOutput, calls=%fused_computation.23.clone.1 | convolution fusion | flops 418375680 | bytes 26797568 | tf_op jit(solution)/shard_map/while/body/eval_jaxpr/gyx,uyx->ygu/dot_general | solution.py:76
  306.9 7.2 %multiply_convert_fusion.6 = bf16[12,512,512]{1,2,0:T(8,128)(2,1)S(1)} fusion(f32[12,512,512]{1,2,0:T(8,128)} %get-tuple-element.391, f32[12,512,512]{1,2,0:T(8,128)S(1)} %fusion.135, f32[12,512]{1,0:T(8,128)S(1)} %get-tuple-element.392, f32[12,512]{1,0:T(8,128)S(1)} %dynamic-slice_bitcast_fusion.6, pred[512]{0:T(512)(128)(4,1)S(1)} %iota_compare_fusion.5), kind=kLoop, calls=%fused_computation.22.clone.1 | loop fusion | flops 18874368 | bytes 31506944 | tf_op jit(solution)/shard_map/while/body/eval_jaxpr/convert_element_type | solution.py:80
  326.8 7.3 %multiply_reduce_fusion.10 = (f32[12,512]{1,0:T(8,128)S(1)}, f32[12,512,512]{1,2,0:T(8,128)}) fusion(f32[12,512,512]{1,2,0:T(8,128)S(1)} %fusion.135, f32[12,512]{1,0:T(8,128)S(1)} %dynamic-slice_bitcast_fusion.6, pred[512]{0:T(512)(128)(4,1)S(1)} %iota_compare_fusion.5, bf16[2,512,12,64]{1,3,2,0:T(8,128)(2,1)S(1)} %copy-done.6, ...), kind=kOutput, calls=%fused_computation.23.clone.1 | convolution fusion | flops 418375680 | bytes 26797568 | tf_op jit(solution)/shard_map/while/body/eval_jaxpr/gyx,uyx->ygu/dot_general | solution.py:76
  334.1 7.2 %multiply_convert_fusion.6 = bf16[12,512,512]{1,2,0:T(8,128)(2,1)S(1)} fusion(f32[12,512,512]{1,2,0:T(8,128)} %get-tuple-element.391, f32[12,512,512]{1,2,0:T(8,128)S(1)} %fusion.135, f32[12,512]{1,0:T(8,128)S(1)} %get-tuple-element.392, f32[12,512]{1,0:T(8,128)S(1)} %dynamic-slice_bitcast_fusion.6, pred[512]{0:T(512)(128)(4,1)S(1)} %iota_compare_fusion.5), kind=kLoop, calls=%fused_computation.22.clone.1 | loop fusion | flops 18874368 | bytes 31506944 | tf_op jit(solution)/shard_map/while/body/eval_jaxpr/convert_element_type | solution.py:80
  380.8 7.7 %reduce-scatter.5.cloned.1.call-done = bf16[1,192,768]{2,1,0:T(8,128)(2,1)} async-done(((bf16[2,192,768]{2,1,0:T(8,128)(2,1)}), bf16[1,192,768]{2,1,0:T(8,128)(2,1)}) %reduce-scatter.5.cloned.1.call-update) | async-done | bytes 294928 | tf_op jit(solution)/shard_map/reduce_scatter | solution.py:157
  388.5 30.6 %reduce-scatter.7.cloned.1.call-done = bf16[1,192,2304]{2,1,0:T(8,128)(2,1)} async-done(((bf16[2,192,2304]{2,1,0:T(8,128)(2,1)}), bf16[1,192,2304]{2,1,0:T(8,128)(2,1)}) %reduce-scatter.7.cloned.1.call-update) | async-done | bytes 884752 | tf_op jit(solution)/shard_map/reduce_scatter | solution.py:157
  419.1 112.7 %all-reduce.7.cloned.1.call-done = (bf16[192,3072]{1,0:T(8,128)(2,1)}, bf16[768,768]{1,0:T(8,128)(2,1)}) async-done(((bf16[192,3072]{1,0:T(8,128)(2,1)}, bf16[768,768]{1,0:T(8,128)(2,1)}), (bf16[192,3072]{1,0:T(8,128)(2,1)}, bf16[768,768]{1,0:T(8,128)(2,1)})) %all-reduce.7.cloned.1.call-update) | async-done | bytes 2359312 | tf_op jit(solution)/shard_map/psum | solution.py:161
  531.9 40.9 %psum.39 = f32[2,4608]{1,0:T(2,128)S(1)} all-reduce(f32[2,4608]{1,0:T(2,128)S(1)} %constant_dynamic-update-slice_fusion.3), channel_id=1, replica_groups=mesh['fsdp'=2,'dp'=16] {'fsdp','dp'}, use_global_device_ids=true, to_apply=%region_31.32 | all-reduce | flops 9216 | bytes 73728 | tf_op jit(solution)/shard_map/psum | solution.py:172
  574.1 10.0 %convolution_add_fusion.1 = f32[1024,768]{1,0:T(8,128)} fusion(f32[1024,768]{1,0:T(8,128)} %copy-done.22, bf16[1024,2304]{0,1:T(8,128)(2,1)} %copy-done.12, bf16[768,2304]{1,0:T(8,128)(2,1)} %bitcast.286), kind=kOutput, calls=%fused_computation.130 | convolution fusion | flops 3624665088 | bytes 14548992 | tf_op jit(solution)/shard_map/dot_general | solution.py:26
  584.1 31.7 %all-reduce.5.cloned.1.call-done = (bf16[192,2304]{1,0:T(8,128)(2,1)}, bf16[192,768]{1,0:T(8,128)(2,1)}) async-done(((bf16[192,2304]{1,0:T(8,128)(2,1)}, bf16[192,768]{1,0:T(8,128)(2,1)}), (bf16[192,2304]{1,0:T(8,128)(2,1)}, bf16[192,768]{1,0:T(8,128)(2,1)})) %all-reduce.5.cloned.1.call-update) | async-done | bytes 1179664 | tf_op jit(solution)/shard_map/psum | solution.py:161
  (360 shorter events, 182.9 us)
Async XLA Ops:
  7.2 36.5 %all-gather.10.cloned.1.call-start = ((), (), s32[]{:S(2)}) async-start(), calls=%async_computation.8 | async-start | bytes 2654208 | tf_op jit(solution)/shard_map/all_gather | solution.py:129
  9.6 73.9 %all-gather.12.cloned.1.call-start = ((), (), s32[]{:S(2)}) async-start(), calls=%async_computation.9 | async-start | bytes 3538944 | tf_op jit(solution)/shard_map/all_gather | solution.py:129
  10.8 36.1 %copy-start.8 = (bf16[2,512,768]{2,1,0:T(8,128)(2,1)S(1)}, bf16[2,512,768]{2,1,0:T(8,128)(2,1)}, u32[]{:S(2)}) copy-start(bf16[2,512,768]{2,1,0:T(8,128)(2,1)} %param.39) | copy-start | bytes 4718596
  10.8 110.8 %all-gather.14.cloned.1.call-start = ((), (), s32[]{:S(2)}) async-start(), calls=%async_computation.10 | async-start | bytes 3538944 | tf_op jit(solution)/shard_map/all_gather | solution.py:129
  13.4 362.9 %reduce-scatter.11.cloned.1.call-start = ((), (), s32[]{:S(2)}) async-start(), calls=%async_computation.7 | async-start | bytes 3538944 | tf_op jit(solution)/shard_map/reduce_scatter | solution.py:157
  26.9 22.5 %collective-permute-start.1 = (bf16[2,192,768]{2,1,0:T(8,128)(2,1)S(1)}, bf16[2,192,768]{2,1,0:T(8,128)(2,1)S(1)}, u32[]{:S(2)}, u32[]{:S(2)}) collective-permute-start(bf16[2,192,768]{2,1,0:T(8,128)(2,1)S(1)} %bitcast.289), channel_id=1, source_target_pairs={{0,1},{1,0},{2,3},{3,2},{4,5},{5,4},{6,7},{7,6},{8,9},{9,8},{10,11... | collective-permute-start | bytes 1769480 | tf_op jit(solution)/shard_map/ppermute | solution.py:130
  43.7 78.0 %collective-permute-start = (bf16[2,192,2304]{2,1,0:T(8,128)(2,1)}, bf16[2,192,2304]{2,1,0:T(8,128)(2,1)}, u32[]{:S(2)}, u32[]{:S(2)}) collective-permute-start(bf16[2,192,2304]{2,1,0:T(8,128)(2,1)} %bitcast.295), channel_id=1, source_target_pairs={{0,1},{1,0},{2,3},{3,2},{4,5},{5,4},{6,7},{7,6},{8,9},{9,8},{10,11... | collective-permute-start | bytes 5308424 | tf_op jit(solution)/shard_map/ppermute | solution.py:130
  49.6 131.0 %copy-start.32 = (bf16[2,2,192,768]{3,2,1,0:T(8,128)(2,1)}, bf16[2,2,192,768]{3,2,1,0:T(8,128)(2,1)S(1)}, u32[]{:S(2)}) copy-start(bf16[2,2,192,768]{3,2,1,0:T(8,128)(2,1)S(1)} %pad_maximum_fusion.6) | copy-start | bytes 3538948
  83.5 99.4 %collective-permute-start.2 = (bf16[2,192,3072]{2,1,0:T(8,128)(2,1)}, bf16[2,192,3072]{2,1,0:T(8,128)(2,1)}, u32[]{:S(2)}, u32[]{:S(2)}) collective-permute-start(bf16[2,192,3072]{2,1,0:T(8,128)(2,1)} %bitcast.291), channel_id=1, source_target_pairs={{0,1},{1,0},{2,3},{3,2},{4,5},{5,4},{6,7},{7,6},{8,9},{9,8},{10,11... | collective-permute-start | bytes 7077896 | tf_op jit(solution)/shard_map/ppermute | solution.py:130
  121.7 65.9 %collective-permute-start.3 = (bf16[2,768,768]{2,1,0:T(8,128)(2,1)}, bf16[2,768,768]{2,1,0:T(8,128)(2,1)}, u32[]{:S(2)}, u32[]{:S(2)}) collective-permute-start(bf16[2,768,768]{2,1,0:T(8,128)(2,1)} %bitcast.293), channel_id=1, source_target_pairs={{0,1},{1,0},{2,3},{3,2},{4,5},{5,4},{6,7},{7,6},{8,9},{9,8},{10,11... | collective-permute-start | bytes 7077896 | tf_op jit(solution)/shard_map/ppermute | solution.py:130
  229.6 19.1 %collective-permute-start.7 = (bf16[2,768,768]{2,1,0:T(8,128)(2,1)S(1)}, bf16[2,768,768]{2,1,0:T(8,128)(2,1)S(1)}, u32[]{:S(2)}, u32[]{:S(2)}) collective-permute-start(bf16[2,768,768]{2,1,0:T(8,128)(2,1)S(1)} %dynamic-slice_bitcast_fusion.1), channel_id=1, source_target_pairs={{0,1},{1,0},{2,3},{3,2},{4,5},{5,4},{6,7},{7,6},{8,9},{9,8},{10,11... | collective-permute-start | bytes 7077896 | tf_op jit(solution)/shard_map/ppermute | solution.py:152
  250.8 125.5 %reduce-scatter.9.cloned.1.call-start = ((), (), s32[]{:S(2)}) async-start(), calls=%async_computation.6 | async-start | bytes 3538944 | tf_op jit(solution)/shard_map/reduce_scatter | solution.py:157
  264.5 21.8 %collective-permute-start.6 = (bf16[2,192,3072]{2,1,0:T(8,128)(2,1)}, bf16[2,192,3072]{2,1,0:T(8,128)(2,1)}, u32[]{:S(2)}, u32[]{:S(2)}) collective-permute-start(bf16[2,192,3072]{2,1,0:T(8,128)(2,1)} %dynamic-slice_bitcast_fusion.2), channel_id=1, source_target_pairs={{0,1},{1,0},{2,3},{3,2},{4,5},{5,4},{6,7},{7,6},{8,9},{9,8},{10,11... | collective-permute-start | bytes 7077896 | tf_op jit(solution)/shard_map/ppermute | solution.py:152
  291.0 97.5 %reduce-scatter.5.cloned.1.call-start = ((), (), s32[]{:S(2)}) async-start(), calls=%async_computation.4 | async-start | bytes 884736 | tf_op jit(solution)/shard_map/reduce_scatter | solution.py:157
  365.9 7.2 %collective-permute-start.5 = (bf16[2,192,2304]{2,1,0:T(8,128)(2,1)}, bf16[2,192,2304]{2,1,0:T(8,128)(2,1)S(1)}, u32[]{:S(2)}, u32[]{:S(2)}) collective-permute-start(bf16[2,192,2304]{2,1,0:T(8,128)(2,1)} %dynamic-slice_bitcast_fusion.3), channel_id=1, source_target_pairs={{0,1},{1,0},{2,3},{3,2},{4,5},{5,4},{6,7},{7,6},{8,9},{9,8},{10,11... | collective-permute-start | bytes 5308424 | tf_op jit(solution)/shard_map/ppermute | solution.py:152
  369.8 2.2 collective-permute-start.4
  373.0 46.1 %reduce-scatter.7.cloned.1.call-start = ((), (), s32[]{:S(2)}) async-start(), calls=%async_computation.5 | async-start | bytes 2654208 | tf_op jit(solution)/shard_map/reduce_scatter | solution.py:157
  376.2 155.6 %all-reduce.7.cloned.1.call-start = ((), (), s32[]{:S(2)}) async-start(), calls=%async_computation.12 | async-start | bytes 4718592 | tf_op jit(solution)/shard_map/psum | solution.py:161
  377.0 238.8 %all-reduce.5.cloned.1.call-start = ((), (), s32[]{:S(2)}) async-start(), calls=%async_computation.11 | async-start | bytes 2359296 | tf_op jit(solution)/shard_map/psum | solution.py:161
  531.8 84.5 %collective-permute-start.10 = (bf16[192,3072]{1,0:T(8,128)(2,1)}, bf16[192,3072]{1,0:T(8,128)(2,1)S(1)}, u32[]{:S(2)}, u32[]{:S(2)}) collective-permute-start(bf16[192,3072]{1,0:T(8,128)(2,1)} %get-tuple-element.120), channel_id=1, source_target_pairs={{0,1},{1,0},{2,3},{3,2},{4,5},{5,4},{6,7},{7,6},{8,9},{9,8},{10,11... | collective-permute-start | bytes 3538952 | tf_op jit(solution)/shard_map/ppermute | solution.py:165
  574.1 42.2 %copy-start.31 = (bf16[192,3072]{1,0:T(8,128)(2,1)S(1)}, bf16[192,3072]{1,0:T(8,128)(2,1)}, u32[]{:S(2)}) copy-start(bf16[192,3072]{1,0:T(8,128)(2,1)} %get-tuple-element.120) | copy-start | bytes 3538948
  584.1 35.5 %collective-permute-start.11 = (bf16[768,768]{1,0:T(8,128)(2,1)S(1)}, bf16[768,768]{1,0:T(8,128)(2,1)}, u32[]{:S(2)}, u32[]{:S(2)}) collective-permute-start(bf16[768,768]{1,0:T(8,128)(2,1)S(1)} %copy-done.30), channel_id=1, source_target_pairs={{0,1},{1,0},{2,3},{3,2},{4,5},{5,4},{6,7},{7,6},{8,9},{9,8},{10,11... | collective-permute-start | bytes 3538952 | tf_op jit(solution)/shard_map/ppermute | solution.py:165
  615.8 8.2 %collective-permute-start.9 = (bf16[192,768]{1,0:T(8,128)(2,1)}, bf16[192,768]{1,0:T(8,128)(2,1)S(1)}, u32[]{:S(2)}, u32[]{:S(2)}) collective-permute-start(bf16[192,768]{1,0:T(8,128)(2,1)} %get-tuple-element.224), channel_id=1, source_target_pairs={{0,1},{1,0},{2,3},{3,2},{4,5},{5,4},{6,7},{7,6},{8,9},{9,8},{10,11... | collective-permute-start | bytes 884744 | tf_op jit(solution)/shard_map/ppermute | solution.py:165
  615.8 9.4 %collective-permute-start.8 = (bf16[192,2304]{1,0:T(8,128)(2,1)}, bf16[192,2304]{1,0:T(8,128)(2,1)S(1)}, u32[]{:S(2)}, u32[]{:S(2)}) collective-permute-start(bf16[192,2304]{1,0:T(8,128)(2,1)} %get-tuple-element.223), channel_id=1, source_target_pairs={{0,1},{1,0},{2,3},{3,2},{4,5},{5,4},{6,7},{7,6},{8,9},{9,8},{10,11... | collective-permute-start | bytes 2654216 | tf_op jit(solution)/shard_map/ppermute | solution.py:165
  (78 other events, 483.3 us)
Sparse Core Ops, SparseCore 0:
  10.2 33.5 all-gather.9
  45.8 37.5 all-gather.11
  85.6 36.0 all-gather.13
  250.9 34.7 reduce-scatter.10
  291.1 34.8 reduce-scatter.8
  373.2 15.3 reduce-scatter.4
  390.9 28.2 reduce-scatter.6
  422.7 109.0 all-reduce.6
  535.8 80.0 all-reduce.4

commit v2 on v1

--- a/solution.py
+++ b/solution.py
@@ -122,13 +122,26 @@
     return jnp.stack([jnp.where(lower, mine, theirs), jnp.where(lower, theirs, mine)], axis=-3)
 
 
-def gather_weight(shard):
-    rows, columns = shard.shape
-    half = rows // 2
-    mine = lax.dynamic_slice_in_dim(shard, own_core() * half, half, axis=0)
-    mine = lax.all_gather(mine, "fsdp", axis=0, tiled=False)
-    theirs = lax.ppermute(mine, "dp", core_pairs())
-    return join_cores(mine, theirs).reshape(-1, columns)
+def row_pairs(distance):
+    return [(index, index ^ distance) for index in range(lax.axis_size("fsdp"))]
+
+
+def gather_halves(shard):
+    half = shard.shape[0] // 2
+    mine = lax.dynamic_slice_in_dim(shard, own_core() * half, half, axis=0)[None]
+    distance = 1
+    while distance < lax.axis_size("fsdp"):
+        theirs = lax.ppermute(mine, "fsdp", row_pairs(distance))
+        lower = lax.rem(lax.axis_index("fsdp") // distance, 2) == 0
+        mine = jnp.concatenate(
+            [jnp.where(lower, mine, theirs), jnp.where(lower, theirs, mine)], axis=0
+        )
+        distance *= 2
+    return mine, lax.ppermute(mine, "dp", core_pairs())
+
+
+def join_weight(halves):
+    return join_cores(*halves).reshape(-1, halves[0].shape[-1])
 
 
 def gather_vectors(vectors):
@@ -153,8 +166,17 @@
     ).astype(jnp.bfloat16)
 
 
-def scatter_weight(grad):
-    return lax.psum_scatter(core_sum(grad), "fsdp", scatter_dimension=0, tiled=False)
+def scatter_weight(part):
+    distance = lax.axis_size("fsdp") // 2
+    while distance >= 1:
+        bit = lax.rem(lax.axis_index("fsdp") // distance, 2)
+        cut = part.reshape(2, distance, *part.shape[1:])
+        kept = lax.dynamic_index_in_dim(cut, bit, axis=0, keepdims=False)
+        sent = lax.dynamic_index_in_dim(cut, 1 - bit, axis=0, keepdims=False)
+        theirs = lax.ppermute(sent, "fsdp", row_pairs(distance))
+        part = (kept.astype(jnp.float32) + theirs.astype(jnp.float32)).astype(jnp.bfloat16)
+        distance //= 2
+    return part[0]
 
 
 def sum_replicas(parts):
@@ -166,14 +188,16 @@
     return join_cores(part, theirs).reshape(-1, part.shape[-1]).astype(jnp.float32)
 
 
-def sum_vectors(grads):
+def pack_vectors(grads):
     groups = lax.axis_size("fsdp")
     packed = jnp.concatenate([grad.reshape(groups, -1) for grad in grads], axis=1)
-    packed = lax.psum(packed, ("fsdp", "dp"))
-    mine = lax.dynamic_index_in_dim(packed, lax.axis_index("fsdp"), axis=0, keepdims=False)
+    return scatter_weight(core_sum(packed.reshape(2 * groups, -1)))
+
+
+def unpack_vectors(mine, grads):
     pieces, start = [], 0
     for grad in grads:
-        size = grad.shape[0] // groups
+        size = grad.shape[0] // lax.axis_size("fsdp")
         pieces.append(mine[start : start + size])
         start += size
     return pieces
@@ -217,7 +241,8 @@
     token_rows = seq_count * seq_len
     heads_shape = (seq_count, seq_len, HEADS, width // HEADS)
     rows_in = hidden_in.reshape(token_rows, width)
-    full_qkv = gather_weight(jnp.concatenate([query_w, key_w, value_w], axis=1))
+    qkv_halves = gather_halves(jnp.concatenate([query_w, key_w, value_w], axis=1))
+    full_qkv = join_weight(qkv_halves)
     (
         full_query_b,
         full_value_b,
@@ -231,16 +256,22 @@
     ) = gather_vectors(
         [query_b, value_b, out_b, gain_one, shift_one, up_b, down_b, gain_two, shift_two]
     )
-    full_out = gather_weight(out_w)
-    full_up = gather_weight(up_w)
-    full_down = gather_weight(down_w)
+    _, up_shard, down_shard, out_shard = lax.optimization_barrier(
+        (qkv_halves[0], up_w, down_w, out_w)
+    )
+    later_halves = tuple(gather_halves(shard) for shard in (out_shard, up_shard, down_shard))
     qkv_bias = jnp.concatenate([full_query_b, jnp.zeros_like(full_query_b), full_value_b])
     qkv = (product(rows_in, full_qkv) + qkv_bias).astype(jnp.bfloat16)
     query_vectors, key_vectors, value_vectors = (
         part.reshape(heads_shape) for part in jnp.split(qkv, 3, axis=1)
     )
-    mixed, log_total = lax.map(attend_one, (query_vectors, key_vectors, value_vectors, lengths))
-    mixed_flat = mixed.reshape(token_rows, width)
+    forward = [
+        attend_one((query_vectors[seq], key_vectors[seq], value_vectors[seq], lengths[seq]))
+        for seq in range(seq_count)
+    ]
+    mixed_flat = jnp.concatenate([mixed for mixed, _ in forward]).reshape(token_rows, width)
+    mixed_flat, later_halves = lax.optimization_barrier((mixed_flat, later_halves))
+    full_out, full_up, full_down = (join_weight(halves) for halves in later_halves)
     branch = product(mixed_flat, full_out) + full_out_b
     normed_one, inverse_one = normalize(rows_in.astype(jnp.float32) + branch)
     first = normed_one * full_gain_one + full_shift_one
@@ -259,38 +290,78 @@
     grad_shift_two = jnp.sum(grad_top, axis=0)
     grad_sum_two = norm_back(grad_top * full_gain_two, normed_two, inverse_two)
     grad_second = grad_sum_two.astype(jnp.bfloat16)
-    part_down = scatter_weight(trans_left(hidden_low, grad_second))
+    core_down = core_sum(trans_left(hidden_low, grad_second))
     grad_down_b = jnp.sum(grad_second.astype(jnp.float32), axis=0)
     grad_hidden = trans_right(grad_second, full_down)
     grad_inner = (grad_hidden * slope_low.astype(jnp.float32)).astype(jnp.bfloat16)
-    part_up = scatter_weight(trans_left(first_low, grad_inner))
+    grad_inner, core_down = lax.optimization_barrier((grad_inner, core_down))
+    part_down = scatter_weight(core_down)
+    core_up = core_sum(trans_left(first_low, grad_inner))
     grad_up_b = jnp.sum(grad_inner.astype(jnp.float32), axis=0)
-    part_up, part_down = sum_replicas((part_up, part_down))
     grad_first = grad_sum_two + trans_right(grad_inner, full_up)
+    grad_first, part_down = lax.optimization_barrier((grad_first, part_down))
+    part_down = sum_replicas(part_down)
     grad_gain_one = jnp.sum(grad_first * normed_one, axis=0)
     grad_shift_one = jnp.sum(grad_first, axis=0)
     grad_sum_one = norm_back(grad_first * full_gain_one, normed_one, inverse_one)
     grad_branch = grad_sum_one.astype(jnp.bfloat16)
-    part_out = scatter_weight(trans_left(mixed_flat, grad_branch))
+    core_out = core_sum(trans_left(mixed_flat, grad_branch))
     grad_out_b = jnp.sum(grad_branch.astype(jnp.float32), axis=0)
     grad_mixed = trans_right(grad_branch, full_out).astype(jnp.bfloat16)
-    grad_query, grad_keys, grad_values = lax.map(
-        attend_back,
-        (
-            query_vectors,
-            key_vectors,
-            value_vectors,
-            lengths,
-            log_total,
-            grad_mixed.reshape(heads_shape),
-        ),
-    )
+    grad_mixed, core_up = lax.optimization_barrier((grad_mixed, core_up))
+    part_up = scatter_weight(core_up)
+    grad_context = grad_mixed.reshape(heads_shape)
+    backward = []
+    for seq in range(seq_count):
+        context_rows = grad_context[seq]
+        if seq == 1:
+            context_rows, backward, part_up = lax.optimization_barrier(
+                (context_rows, backward, part_up)
+            )
+        backward.append(
+            attend_back(
+                (
+                    query_vectors[seq],
+                    key_vectors[seq],
+                    value_vectors[seq],
+                    lengths[seq],
+                    forward[seq][1],
+                    context_rows,
+                )
+            )
+        )
+    part_out = scatter_weight(core_out)
     grad_qkv = jnp.concatenate(
-        [part.reshape(token_rows, width) for part in (grad_query, grad_keys, grad_values)], axis=1
-    )
+        [
+            jnp.concatenate([part.reshape(seq_len, width) for part in parts], axis=1)
+            for parts in backward
+        ]
+    )
+    grad_qkv, part_out, part_up, part_down = lax.optimization_barrier(
+        (grad_qkv, part_out, part_up, part_down)
+    )
+    part_up = sum_replicas(part_up)
     grad_qkv_b = jnp.sum(grad_qkv.astype(jnp.float32), axis=0)
-    part_qkv = scatter_weight(trans_left(rows_in, grad_qkv))
+    part_qkv = core_sum(trans_left(rows_in, grad_qkv))
     grad_in = grad_sum_one + trans_right(grad_qkv, full_qkv)
+    vector_grads = [
+        grad_qkv_b[:width],
+        grad_qkv_b[2 * width :],
+        grad_out_b,
+        grad_gain_one,
+        grad_shift_one,
+        grad_up_b,
+        grad_down_b,
+        grad_gain_two,
+        grad_shift_two,
+    ]
+    part_vectors = pack_vectors(vector_grads)
+    part_out, part_qkv, part_up, part_down = lax.optimization_barrier(
+        (part_out, part_qkv, part_up, part_down)
+    )
+    part_out, part_qkv, part_vectors = sum_replicas(
+        (part_out, scatter_weight(part_qkv), part_vectors)
+    )
     (
         own_query_b,
         own_value_b,
@@ -301,23 +372,7 @@
         own_down_b,
         own_gain_two,
         own_shift_two,
-    ) = sum_vectors(
-        [
-            grad_qkv_b[:width],
-            grad_qkv_b[2 * width :],
-            grad_out_b,
-            grad_gain_one,
-            grad_shift_one,
-            grad_up_b,
-            grad_down_b,
-            grad_gain_two,
-            grad_shift_two,
-        ]
-    )
-    part_out, part_qkv, part_up, part_down = lax.optimization_barrier(
-        (part_out, part_qkv, part_up, part_down)
-    )
-    part_out, part_qkv = sum_replicas((part_out, part_qkv))
+    ) = unpack_vectors(both_cores(part_vectors).reshape(-1), vector_grads)
     own_up_w, own_down_w, own_out_w, own_qkv_w = (
         both_cores(part) for part in (part_up, part_down, part_out, part_qkv)
     )

time: 643 us -> 609 us (0.947)
  waiting for transfers between devices: 267 us -> 209 us
  other arithmetic: 65.2 us -> 116 us
  blocking collectives: 59.6 us -> 35.7 us
  local copies, waits for them, and re-layouts: 80.4 us -> 63.8 us
  starting transfers between devices: 2.97 us -> 15.9 us
    all_gather x3 -> x0, waiting for transfers between devices: 81.5 us -> none  [gather_weight(): mine = lax.all_gather(mine, 'fsdp', axis=0, tiled=False)]
    ppermute x4 -> x13, waiting for transfers between devices: 0.01 us -> 81.3 us  [the longest x4 47.6 us: gather_halves(): theirs = lax.ppermute(mine, 'fsdp', row_pairs(distance))]
    reduce_scatter x4 -> x0, waiting for transfers between devices: 38.4 us -> none  [scatter_weight(): lax.psum_scatter(core_sum(grad), 'fsdp', scatter_dimension=0, tiled=False)]
    concatenate x1 -> x6, other arithmetic: 2.26 us -> 33.3 us  [the longest x1 29 us: shards(): jnp.concatenate([jnp.concatenate([part.reshape(seq_len, width) for part i...]
    while x40 -> x0, local copies, waits for them, and re-layouts: 24.1 us -> none  [the longest x4 11.1 us: shards(): lax.map(attend_one, (query_vectors, key_vectors, value_vectors, lengths))]
    psum x1, blocking collectives: 40.9 us -> 23.3 us  [sum_replicas(): return lax.psum(parts, 'dp', axis_index_groups=same_core_groups())]
    psum x2 -> x3, waiting for transfers between devices: 144 us -> 128 us  [sum_replicas(): return lax.psum(parts, 'dp', axis_index_groups=same_core_groups())]
    ppermute x4 -> x13, starting transfers between devices: 0.06 us -> 13.9 us  [the longest x4 6.9 us: gather_halves(): theirs = lax.ppermute(mine, 'fsdp', row_pairs(distance))]
  transfers between devices with their start and end apart: 21 -> 26, of which waited for: 8 -> 7; matrix products, arithmetic and copies ran while one was open for 36% -> 38% of each run, Pallas kernels for 0% -> 0%
where the time goes in v2:
time: 609 us; the launch traced here: 602 us
  waiting for transfers between devices  209 us (34%)
  matrix products  146 us (24%)
  other arithmetic  116 us (19%)
  local copies, waits for them, and re-layouts  63.8 us (10%)
  blocking collectives  35.7 us (6%)
  starting transfers between devices  15.9 us (3%)
  between operations  15.3 us (3%)
    psum x3, waiting for transfers between devices, sum_replicas(): return lax.psum(parts, 'dp', axis_index_groups=same_core_groups())  128 us
    ppermute x4, waiting for transfers between devices, gather_halves(): theirs = lax.ppermute(mine, 'fsdp', row_pairs(distance))  47.6 us
    dot_general x4, matrix products, trans_right(): lax.dot_general(left, right, (((1,), (1,)), ((), ())), preferred_element_...  34.3 us
    ppermute x5, waiting for transfers between devices, scatter_weight(): theirs = lax.ppermute(sent, 'fsdp', row_pairs(distance))  33.7 us
    unnamed x168, local copies, waits for them, and re-layouts  31.1 us
    dot_general x4, matrix products, product(): return jnp.dot(left, right, preferred_element_type=jnp.float32)  29.5 us
    concatenate x1, other arithmetic, shards(): jnp.concatenate([jnp.concatenate([part.reshape(seq_len, width) for part i...  29 us
    psum x1, blocking collectives, sum_replicas(): return lax.psum(parts, 'dp', axis_index_groups=same_core_groups())  23.3 us
  transfers between devices with their start and end apart: 26, of which 7 were waited for; matrix products, arithmetic and copies ran while one was open for 38% of the time, Pallas kernels for 0%

profile of v2, /device:TPU:0, one launch (start us, length us, event | category | flops | bytes accessed | tf_op | source)
XLA Modules:
  0.0 602.4 jit_solution(18428842804687465883)
XLA Ops:
  19.3 12.3 %all-gather.1 = bf16[2,1,4608]{2,1,0:T(2,128)(2,1)S(1)} all-gather(bf16[1,1,4608]{2,1,0:T(2,128)(2,1)S(1)} %reshape.466), channel_id=2, replica_groups=mesh['fsdp'=2,'dp'=16] {'fsdp'}, dimensions={0}, use_global_device_ids=true | all-gather | bytes 27648 | tf_op jit(solution)/shard_map/all_gather | solution.py:148
  47.2 27.5 %collective-permute-done.2 = bf16[1,192,768]{2,1,0:T(8,128)(2,1)} collective-permute-done((bf16[1,192,768]{2,1,0:T(8,128)(2,1)S(1)}, bf16[1,192,768]{2,1,0:T(8,128)(2,1)}, u32[]{:S(2)}, u32[]{:S(2)}) %collective-permute-start.2) | collective-permute-done | bytes 294944 | tf_op jit(solution)/shard_map/ppermute | solution.py:134
  78.2 20.0 %collective-permute-done.6 = bf16[1,768,768]{2,1,0:T(8,128)(2,1)S(1)} collective-permute-done((bf16[1,768,768]{2,1,0:T(8,128)(2,1)S(1)}, bf16[1,768,768]{2,1,0:T(8,128)(2,1)S(1)}, u32[]{:S(2)}, u32[]{:S(2)}) %collective-permute-start.6) | collective-permute-done | bytes 1179680 | tf_op jit(solution)/shard_map/ppermute | solution.py:134
  144.3 17.3 %multiply_convert_fusion.3 = (bf16[1024,3072]{1,0:T(8,128)(2,1)S(1)}, f32[1024,3072]{1,0:T(8,128)}) fusion(f32[3072]{0:T(1024)S(1)} %reshape.449, bf16[768,3072]{1,0:T(8,128)(2,1)S(1)} %bitcast.235, f32[1024,768]{1,0:T(8,128)S(1)} %get-tuple-element.154, f32[768]{0:T(1024)S(1)} %reshape.448, f32[768]{0:T(1024)S(1)} %reshape.447, ...), kind=kOutput, calls=%fused_computation.15 | convolution fusion | flops 4908122112 | bytes 26765312 | tf_op jit(solution)/shard_map/dot_general | solution.py:16
  161.6 5.4 fusion.69
  172.5 5.8 convolution_convert_fusion.1
  180.4 16.9 %multiply_convert_fusion.2 = bf16[1024,3072]{1,0:T(8,128)(2,1)S(1)} fusion(bf16[3072,768]{1,0:T(8,128)(2,1)} %bitcast.240, f32[1024,3072]{1,0:T(8,128)} %get-tuple-element.156, f32[3072]{0:T(1024)S(1)} %reshape.449, f32[1024,768]{1,0:T(8,128)S(1)} %get-tuple-element.86), kind=kOutput, calls=%fused_computation.14 | convolution fusion | flops 4920705024 | bytes 26750976 | tf_op jit(solution)/shard_map/dot_general | solution.py:26
  203.2 6.7 %convolution_convert_fusion = bf16[768,3072]{1,0:T(8,128)(2,1)S(1)} fusion(bf16[1024,3072]{1,0:T(8,128)(2,1)S(1)} %multiply_convert_fusion.2, f32[1024,768]{1,0:T(8,128)S(1)} %get-tuple-element.154, f32[768]{0:T(1024)S(1)} %reshape.448, f32[768]{0:T(1024)S(1)} %reshape.447, f32[1024]{0:T(1024)S(1)} %add_rsqrt_fusion.1, f32[1024]{0:T(1024)S(1)} %broadcast_multiply_fusion.4), kind=kOutput, calls=%fused_computation.33 | convolution fusion | flops 4838129664 | bytes 14170112 | tf_op jit(solution)/shard_map/dot_general | solution.py:20
  213.9 6.8 %convolution_add_fusion = f32[1024,768]{1,0:T(8,128)} fusion(f32[1024,768]{1,0:T(8,128)S(1)} %copy-done.29, bf16[1024,3072]{1,0:T(8,128)(2,1)S(1)} %multiply_convert_fusion.2, bf16[768,3072]{1,0:T(8,128)(2,1)S(1)} %bitcast.238), kind=kOutput, calls=%fused_computation.92 | convolution fusion | flops 4832624640 | bytes 17301504 | tf_op jit(solution)/shard_map/dot_general | solution.py:26
  220.6 9.0 %collective-permute-done.9 = bf16[1,768,768]{2,1,0:T(8,128)(2,1)S(1)} collective-permute-done((bf16[1,768,768]{2,1,0:T(8,128)(2,1)S(1)}, bf16[1,768,768]{2,1,0:T(8,128)(2,1)S(1)}, u32[]{:S(2)}, u32[]{:S(2)}) %collective-permute-start.9) | collective-permute-done | bytes 1179680 | tf_op jit(solution)/shard_map/ppermute | solution.py:176
  251.8 5.3 collective-permute-done.13
  265.7 11.4 %multiply_reduce_fusion.1 = (f32[12,512]{1,0:T(8,128)S(1)}, f32[12,512,512]{1,2,0:T(8,128)}) fusion(f32[12,512,512]{1,2,0:T(8,128)} %copy-done.1, f32[12,512]{1,0:T(8,128)S(1)} %log_add_fusion.1, bf16[512,12,64]{0,2,1:T(8,128)(2,1)S(1)} %bitcast.221, bf16[512,12,64]{0,2,1:T(8,128)(2,1)} %bitcast.248), kind=kOutput, calls=%fused_computation.12 | convolution fusion | flops 412084224 | bytes 26787840 | tf_op jit(solution)/shard_map/gyx,uyx->ygu/dot_general | solution.py:76
  278.9 6.9 %multiply_convert_fusion.1 = bf16[12,512,512]{1,2,0:T(8,128)(2,1)S(1)} fusion(f32[12,512,512]{1,2,0:T(8,128)} %get-tuple-element.160, f32[12,512,512]{1,2,0:T(8,128)S(1)} %bitcast.214, f32[12,512]{1,0:T(8,128)S(1)} %get-tuple-element.159, f32[12,512]{1,0:T(8,128)S(1)} %log_add_fusion.1), kind=kLoop, calls=%fused_computation.11 | loop fusion | flops 12582912 | bytes 31506432 | tf_op jit(solution)/shard_map/convert_element_type | solution.py:80
  296.0 7.5 %fusion.33 = bf16[512,12,64]{0,2,1:T(8,128)(2,1)} fusion(bf16[512,12,64]{0,2,1:T(8,128)(2,1)S(1)} %bitcast.222, f32[12,512,512]{1,2,0:T(8,128)} %copy-done.1, f32[12,512]{1,0:T(8,128)S(1)} %log_add_fusion.1), kind=kOutput, calls=%fused_computation.105 | convolution fusion | flops 409337856 | bytes 14180352 | tf_op jit(solution)/shard_map/ygu,gyp->uyp/dot_general | solution.py:93
  306.3 10.7 %multiply_reduce_fusion = (f32[12,512]{1,0:T(8,128)S(1)}, f32[12,512,512]{1,2,0:T(8,128)}) fusion(f32[12,512,512]{1,2,0:T(8,128)} %copy-done, f32[12,512]{1,0:T(8,128)S(1)} %log_add_fusion, bf16[512,12,64]{0,2,1:T(8,128)(2,1)S(1)} %bitcast.219, bf16[512,12,64]{0,2,1:T(8,128)(2,1)} %bitcast.246), kind=kOutput, calls=%fused_computation.9 | convolution fusion | flops 412084224 | bytes 26787840 | tf_op jit(solution)/shard_map/gyx,uyx->ygu/dot_general | solution.py:76
  317.0 7.0 %fusion.28 = bf16[12,64,512]{2,1,0:T(8,128)(2,1)S(1)} fusion(bf16[512,12,64]{0,2,1:T(8,128)(2,1)S(1)} %bitcast.220, f32[12,512,512]{1,2,0:T(8,128)} %copy-done, f32[12,512]{1,0:T(8,128)S(1)} %log_add_fusion), kind=kOutput, calls=%fused_computation.102 | convolution fusion | flops 409337856 | bytes 14180352 | tf_op jit(solution)/shard_map/ygu,gyp->uyp/dot_general | solution.py:93
  324.0 7.1 %multiply_convert_fusion = bf16[12,512,512]{1,2,0:T(8,128)(2,1)S(1)} fusion(f32[12,512,512]{1,2,0:T(8,128)} %get-tuple-element.162, f32[12,512,512]{1,2,0:T(8,128)S(1)} %bitcast.212, f32[12,512]{1,0:T(8,128)S(1)} %get-tuple-element.161, f32[12,512]{1,0:T(8,128)S(1)} %log_add_fusion), kind=kLoop, calls=%fused_computation.8 | loop fusion | flops 12582912 | bytes 31506432 | tf_op jit(solution)/shard_map/convert_element_type | solution.py:80
  334.4 29.0 %maximum_maximum_fusion = bf16[1024,2304]{0,1:T(8,128)(2,1)} fusion(bf16[512,768]{0,1:T(8,128)(2,1)S(1)} %bitcast.250, bf16[512,768]{0,1:T(8,128)(2,1)S(1)} %bitcast.252, bf16[512,768]{0,1:T(8,128)(2,1)S(1)} %bitcast.228, bf16[512,768]{0,1:T(8,128)(2,1)S(1)} %bitcast.249, bf16[512,768]{0,1:T(8,128)(2,1)S(1)} %bitcast.251, bf16[512,768]{0,1:T(8,128)(2,1)S(1)} %bitcast.227), kind=kLoop, calls=%fused_computation.39 | loop fusion | flops 28311552 | bytes 9437184 | tf_op jit(solution)/shard_map/concatenate | solution.py:334
  363.4 7.9 %convolution_convert_fusion.2 = bf16[2304,768]{0,1:T(8,128)(2,1)} fusion(bf16[1024,2304]{0,1:T(8,128)(2,1)} %maximum_maximum_fusion, bf16[1024,768]{1,0:T(8,128)(2,1)S(1)} %bitcast.267), kind=kOutput, calls=%fused_computation.35 | convolution fusion | flops 3625648128 | bytes 9830400 | tf_op jit(solution)/shard_map/dot_general | solution.py:20
  393.1 7.9 %convolution_add_fusion.1 = f32[1024,768]{1,0:T(8,128)} fusion(f32[1024,768]{1,0:T(8,128)S(1)} %copy-done.33, bf16[1024,2304]{0,1:T(8,128)(2,1)} %maximum_maximum_fusion, bf16[768,2304]{1,0:T(8,128)(2,1)S(1)} %bitcast.242), kind=kOutput, calls=%fused_computation.93 | convolution fusion | flops 3624665088 | bytes 14548992 | tf_op jit(solution)/shard_map/dot_general | solution.py:26
  401.9 23.3 %psum.39 = bf16[1,2304]{1,0:T(2,128)(2,1)S(1)} all-reduce(bf16[1,2304]{1,0:T(2,128)(2,1)S(1)} %convert_bitcast_fusion), channel_id=1, replica_groups={{0,2,4,6,8,10,12,14},{1,3,5,7,9,11,13,15},{16,18,20,22,24,26,28,30},{17..., use_global_device_ids=true, to_apply=%region_26.27 | all-reduce | flops 2304 | bytes 9216 | tf_op jit(solution)/shard_map/psum | solution.py:183
  427.7 55.3 %all-reduce.7.cloned.1.call-done = bf16[192,3072]{1,0:T(8,128)(2,1)} async-done(((bf16[192,3072]{1,0:T(8,128)(2,1)}), bf16[192,3072]{1,0:T(8,128)(2,1)}) %all-reduce.7.cloned.1.call-update) | async-done | bytes 1179664 | tf_op jit(solution)/shard_map/psum | solution.py:183
  487.1 19.3 %collective-permute-done.15 = bf16[1,192,2304]{2,1,0:T(8,128)(2,1)} collective-permute-done((bf16[1,192,2304]{2,1,0:T(8,128)(2,1)}, bf16[1,192,2304]{2,1,0:T(8,128)(2,1)}, u32[]{:S(2)}, u32[]{:S(2)}) %collective-permute-start.15) | collective-permute-done | bytes 884768 | tf_op jit(solution)/shard_map/ppermute | solution.py:176
  516.0 72.6 %all-reduce.9.cloned.1.call-done = (bf16[192,2304]{1,0:T(8,128)(2,1)}, bf16[192,768]{1,0:T(8,128)(2,1)}) async-done(((bf16[192,2304]{1,0:T(8,128)(2,1)}, bf16[192,768]{1,0:T(8,128)(2,1)}), (bf16[192,2304]{1,0:T(8,128)(2,1)}, bf16[192,768]{1,0:T(8,128)(2,1)})) %all-reduce.9.cloned.1.call-update) | async-done | bytes 1179664 | tf_op jit(solution)/shard_map/psum | solution.py:183
  (346 shorter events, 187.7 us)
Async XLA Ops:
  7.2 356.2 %all-reduce.5.cloned.1.call-start = ((), (), s32[]{:S(2)}) async-start(), calls=%async_computation | async-start | bytes 2359296 | tf_op jit(solution)/shard_map/psum | solution.py:183
  8.6 26.4 %collective-permute-start = (bf16[1,192,2304]{2,1,0:T(8,128)(2,1)S(1)}, bf16[1,192,2304]{2,1,0:T(8,128)(2,1)}, u32[]{:S(2)}, u32[]{:S(2)}) collective-permute-start(bf16[1,192,2304]{2,1,0:T(8,128)(2,1)S(1)} %fusion.46), channel_id=1, source_target_pairs={{0,16},{16,0},{1,17},{17,1},{2,18},{18,2},{3,19},{19,3},{4,20},{20... | collective-permute-start | bytes 2654216 | tf_op jit(solution)/shard_map/ppermute | solution.py:134
  39.2 37.6 %collective-permute-start.4 = (bf16[1,192,3072]{2,1,0:T(8,128)(2,1)}, bf16[1,192,3072]{2,1,0:T(8,128)(2,1)S(1)}, u32[]{:S(2)}, u32[]{:S(2)}) collective-permute-start(bf16[1,192,3072]{2,1,0:T(8,128)(2,1)} %dynamic-slice_bitcast_fusion.4), channel_id=1, source_target_pairs={{0,16},{16,0},{1,17},{17,1},{2,18},{18,2},{3,19},{19,3},{4,20},{20... | collective-permute-start | bytes 3538952 | tf_op jit(solution)/shard_map/ppermute | solution.py:134
  42.1 32.6 %collective-permute-start.2 = (bf16[1,192,768]{2,1,0:T(8,128)(2,1)S(1)}, bf16[1,192,768]{2,1,0:T(8,128)(2,1)}, u32[]{:S(2)}, u32[]{:S(2)}) collective-permute-start(bf16[1,192,768]{2,1,0:T(8,128)(2,1)S(1)} %dynamic-slice_bitcast_fusion.6), channel_id=1, source_target_pairs={{0,16},{16,0},{1,17},{17,1},{2,18},{18,2},{3,19},{19,3},{4,20},{20... | collective-permute-start | bytes 884744 | tf_op jit(solution)/shard_map/ppermute | solution.py:134
  43.8 56.6 %collective-permute-start.1 = (bf16[2,192,2304]{2,1,0:T(8,128)(2,1)}, bf16[2,192,2304]{2,1,0:T(8,128)(2,1)S(1)}, u32[]{:S(2)}, u32[]{:S(2)}) collective-permute-start(bf16[2,192,2304]{2,1,0:T(8,128)(2,1)} %pad_maximum_fusion.7), channel_id=1, source_target_pairs={{0,1},{1,0},{2,3},{3,2},{4,5},{5,4},{6,7},{7,6},{8,9},{9,8},{10,11... | collective-permute-start | bytes 5308424 | tf_op jit(solution)/shard_map/ppermute | solution.py:140
  45.4 52.9 %collective-permute-start.6 = (bf16[1,768,768]{2,1,0:T(8,128)(2,1)S(1)}, bf16[1,768,768]{2,1,0:T(8,128)(2,1)S(1)}, u32[]{:S(2)}, u32[]{:S(2)}) collective-permute-start(bf16[1,768,768]{2,1,0:T(8,128)(2,1)S(1)} %dynamic-slice_bitcast_fusion.3), channel_id=1, source_target_pairs={{0,16},{16,0},{1,17},{17,1},{2,18},{18,2},{3,19},{19,3},{4,20},{20... | collective-permute-start | bytes 3538952 | tf_op jit(solution)/shard_map/ppermute | solution.py:134
  76.8 54.5 %collective-permute-start.3 = (bf16[2,192,768]{2,1,0:T(8,128)(2,1)}, bf16[2,192,768]{2,1,0:T(8,128)(2,1)}, u32[]{:S(2)}, u32[]{:S(2)}) collective-permute-start(bf16[2,192,768]{2,1,0:T(8,128)(2,1)} %pad_maximum_fusion.11), channel_id=1, source_target_pairs={{0,1},{1,0},{2,3},{3,2},{4,5},{5,4},{6,7},{7,6},{8,9},{9,8},{10,11... | collective-permute-start | bytes 1769480 | tf_op jit(solution)/shard_map/ppermute | solution.py:140
  77.6 53.6 %collective-permute-start.5 = (bf16[2,192,3072]{2,1,0:T(8,128)(2,1)S(1)}, bf16[2,192,3072]{2,1,0:T(8,128)(2,1)}, u32[]{:S(2)}, u32[]{:S(2)}) collective-permute-start(bf16[2,192,3072]{2,1,0:T(8,128)(2,1)S(1)} %pad_maximum_fusion.3), channel_id=1, source_target_pairs={{0,1},{1,0},{2,3},{3,2},{4,5},{5,4},{6,7},{7,6},{8,9},{9,8},{10,11... | collective-permute-start | bytes 7077896 | tf_op jit(solution)/shard_map/ppermute | solution.py:140
  100.4 30.9 %collective-permute-start.7 = (bf16[2,768,768]{2,1,0:T(8,128)(2,1)}, bf16[2,768,768]{2,1,0:T(8,128)(2,1)}, u32[]{:S(2)}, u32[]{:S(2)}) collective-permute-start(bf16[2,768,768]{2,1,0:T(8,128)(2,1)} %pad_maximum_fusion.4), channel_id=1, source_target_pairs={{0,1},{1,0},{2,3},{3,2},{4,5},{5,4},{6,7},{7,6},{8,9},{9,8},{10,11... | collective-permute-start | bytes 7077896 | tf_op jit(solution)/shard_map/ppermute | solution.py:140
  179.9 17.5 %collective-permute-start.8 = (bf16[2,768,768]{2,1,0:T(8,128)(2,1)}, bf16[2,768,768]{2,1,0:T(8,128)(2,1)}, u32[]{:S(2)}, u32[]{:S(2)}) collective-permute-start(bf16[2,768,768]{2,1,0:T(8,128)(2,1)} %dynamic-slice_bitcast_fusion.1), channel_id=1, source_target_pairs={{0,1},{1,0},{2,3},{3,2},{4,5},{5,4},{6,7},{7,6},{8,9},{9,8},{10,11... | collective-permute-start | bytes 7077896 | tf_op jit(solution)/shard_map/ppermute | solution.py:165
  201.7 28.0 %collective-permute-start.9 = (bf16[1,768,768]{2,1,0:T(8,128)(2,1)S(1)}, bf16[1,768,768]{2,1,0:T(8,128)(2,1)S(1)}, u32[]{:S(2)}, u32[]{:S(2)}) collective-permute-start(bf16[1,768,768]{2,1,0:T(8,128)(2,1)S(1)} %constant_dynamic-slice_fusion.4), channel_id=1, source_target_pairs={{0,16},{16,0},{1,17},{17,1},{2,18},{18,2},{3,19},{19,3},{4,20},{20... | collective-permute-start | bytes 3538952 | tf_op jit(solution)/shard_map/ppermute | solution.py:176
  213.8 44.1 %collective-permute-start.10 = (bf16[2,192,3072]{2,1,0:T(8,128)(2,1)}, bf16[2,192,3072]{2,1,0:T(8,128)(2,1)}, u32[]{:S(2)}, u32[]{:S(2)}) collective-permute-start(bf16[2,192,3072]{2,1,0:T(8,128)(2,1)} %dynamic-slice_bitcast_fusion), channel_id=1, source_target_pairs={{0,1},{1,0},{2,3},{3,2},{4,5},{5,4},{6,7},{7,6},{8,9},{9,8},{10,11... | collective-permute-start | bytes 7077896 | tf_op jit(solution)/shard_map/ppermute | solution.py:165
  238.8 7.3 %collective-permute-start.12 = (bf16[2,192,768]{2,1,0:T(8,128)(2,1)}, bf16[2,192,768]{2,1,0:T(8,128)(2,1)}, u32[]{:S(2)}, u32[]{:S(2)}) collective-permute-start(bf16[2,192,768]{2,1,0:T(8,128)(2,1)} %dynamic-slice_bitcast_fusion.5), channel_id=1, source_target_pairs={{0,1},{1,0},{2,3},{3,2},{4,5},{5,4},{6,7},{7,6},{8,9},{9,8},{10,11... | collective-permute-start | bytes 1769480 | tf_op jit(solution)/shard_map/ppermute | solution.py:165
  244.4 238.7 %all-reduce.7.cloned.1.call-start = ((), (), s32[]{:S(2)}) async-start(), calls=%async_computation.1 | async-start | bytes 2359296 | tf_op jit(solution)/shard_map/psum | solution.py:183
  247.6 9.5 %collective-permute-start.13 = (bf16[1,192,768]{2,1,0:T(8,128)(2,1)S(1)}, bf16[1,192,768]{2,1,0:T(8,128)(2,1)S(1)}, u32[]{:S(2)}, u32[]{:S(2)}) collective-permute-start(bf16[1,192,768]{2,1,0:T(8,128)(2,1)S(1)} %constant_dynamic-slice_fusion.2), channel_id=1, source_target_pairs={{0,16},{16,0},{1,17},{17,1},{2,18},{18,2},{3,19},{19,3},{4,20},{20... | collective-permute-start | bytes 884744 | tf_op jit(solution)/shard_map/ppermute | solution.py:176
  261.6 41.9 %collective-permute-start.11 = (bf16[1,192,3072]{2,1,0:T(8,128)(2,1)}, bf16[1,192,3072]{2,1,0:T(8,128)(2,1)}, u32[]{:S(2)}, u32[]{:S(2)}) collective-permute-start(bf16[1,192,3072]{2,1,0:T(8,128)(2,1)} %constant_dynamic-slice_fusion.3), channel_id=1, source_target_pairs={{0,16},{16,0},{1,17},{17,1},{2,18},{18,2},{3,19},{19,3},{4,20},{20... | collective-permute-start | bytes 3538952 | tf_op jit(solution)/shard_map/ppermute | solution.py:176
  390.8 34.5 %collective-permute-start.14 = (bf16[2,192,2304]{2,1,0:T(8,128)(2,1)}, bf16[2,192,2304]{2,1,0:T(8,128)(2,1)}, u32[]{:S(2)}, u32[]{:S(2)}) collective-permute-start(bf16[2,192,2304]{2,1,0:T(8,128)(2,1)} %dynamic-slice_bitcast_fusion.2), channel_id=1, source_target_pairs={{0,1},{1,0},{2,3},{3,2},{4,5},{5,4},{6,7},{7,6},{8,9},{9,8},{10,11... | collective-permute-start | bytes 5308424 | tf_op jit(solution)/shard_map/ppermute | solution.py:165
  392.5 8.5 %collective-permute-start.19 = (bf16[1,1,2304]{2,1,0:T(2,128)(2,1)}, bf16[1,1,2304]{2,1,0:T(2,128)(2,1)S(1)}, u32[]{:S(2)}, u32[]{:S(2)}) collective-permute-start(bf16[1,1,2304]{2,1,0:T(2,128)(2,1)} %constant_dynamic-slice_fusion), channel_id=1, source_target_pairs={{0,16},{16,0},{1,17},{17,1},{2,18},{18,2},{3,19},{19,3},{4,20},{20... | collective-permute-start | bytes 13832 | tf_op jit(solution)/shard_map/ppermute | solution.py:176
  401.0 187.6 %all-reduce.9.cloned.1.call-start = ((), (), s32[]{:S(2)}) async-start(), calls=%async_computation.2 | async-start | bytes 2359296 | tf_op jit(solution)/shard_map/psum | solution.py:183
  425.2 60.3 %collective-permute-start.20 = (bf16[1,2304]{1,0:T(2,128)(2,1)S(1)}, bf16[1,2304]{1,0:T(2,128)(2,1)S(1)}, u32[]{:S(2)}, u32[]{:S(2)}) collective-permute-start(bf16[1,2304]{1,0:T(2,128)(2,1)S(1)} %psum.39), channel_id=1, source_target_pairs={{0,1},{1,0},{2,3},{3,2},{4,5},{5,4},{6,7},{7,6},{8,9},{9,8},{10,11... | collective-permute-start | bytes 13832 | tf_op jit(solution)/shard_map/ppermute | solution.py:187
  483.1 25.7 %collective-permute-start.22 = (bf16[768,768]{1,0:T(8,128)(2,1)S(1)}, bf16[768,768]{1,0:T(8,128)(2,1)}, u32[]{:S(2)}, u32[]{:S(2)}) collective-permute-start(bf16[768,768]{1,0:T(8,128)(2,1)S(1)} %copy-done.40), channel_id=1, source_target_pairs={{0,1},{1,0},{2,3},{3,2},{4,5},{5,4},{6,7},{7,6},{8,9},{9,8},{10,11... | collective-permute-start | bytes 3538952 | tf_op jit(solution)/shard_map/ppermute | solution.py:187
  484.1 22.4 %collective-permute-start.15 = (bf16[1,192,2304]{2,1,0:T(8,128)(2,1)}, bf16[1,192,2304]{2,1,0:T(8,128)(2,1)}, u32[]{:S(2)}, u32[]{:S(2)}) collective-permute-start(bf16[1,192,2304]{2,1,0:T(8,128)(2,1)} %constant_dynamic-slice_fusion.1), channel_id=1, source_target_pairs={{0,16},{16,0},{1,17},{17,1},{2,18},{18,2},{3,19},{19,3},{4,20},{20... | collective-permute-start | bytes 2654216 | tf_op jit(solution)/shard_map/ppermute | solution.py:176
  486.9 23.6 %collective-permute-start.21 = (bf16[192,3072]{1,0:T(8,128)(2,1)}, bf16[192,3072]{1,0:T(8,128)(2,1)}, u32[]{:S(2)}, u32[]{:S(2)}) collective-permute-start(bf16[192,3072]{1,0:T(8,128)(2,1)} %all-reduce.7.cloned.1.call-done), channel_id=1, source_target_pairs={{0,1},{1,0},{2,3},{3,2},{4,5},{5,4},{6,7},{7,6},{8,9},{9,8},{10,11... | collective-permute-start | bytes 3538952 | tf_op jit(solution)/shard_map/ppermute | solution.py:187
  588.6 4.5 collective-permute-start.16
  (76 other events, 677.5 us)
Sparse Core Ops, SparseCore 0:
  244.5 81.4 all-reduce.4
  401.2 81.8 all-reduce.6
  508.9 79.7 all-reduce.8

commit v3 on v2

--- a/solution.py
+++ b/solution.py
@@ -331,16 +331,16 @@
             )
         )
     part_out = scatter_weight(core_out)
-    grad_qkv = jnp.concatenate(
-        [
-            jnp.concatenate([part.reshape(seq_len, width) for part in parts], axis=1)
-            for parts in backward
-        ]
-    )
-    grad_qkv, part_out, part_up, part_down = lax.optimization_barrier(
-        (grad_qkv, part_out, part_up, part_down)
-    )
+    grad_parts = lax.optimization_barrier(
+        tuple(
+            jnp.concatenate([part.reshape(seq_len, width) for part in parts])
+            for parts in zip(*backward)
+        )
+    )
+    grad_qkv = jnp.concatenate(grad_parts, axis=1)
+    part_up, part_down = lax.optimization_barrier((part_up, part_down))
     part_up = sum_replicas(part_up)
+    grad_qkv, part_out, part_down = lax.optimization_barrier((grad_qkv, part_out, part_down))
     grad_qkv_b = jnp.sum(grad_qkv.astype(jnp.float32), axis=0)
     part_qkv = core_sum(trans_left(rows_in, grad_qkv))
     grad_in = grad_sum_one + trans_right(grad_qkv, full_qkv)
@@ -356,12 +356,15 @@
         grad_shift_two,
     ]
     part_vectors = pack_vectors(vector_grads)
+    part_qkv = scatter_weight(part_qkv)
     part_out, part_qkv, part_up, part_down = lax.optimization_barrier(
         (part_out, part_qkv, part_up, part_down)
     )
-    part_out, part_qkv, part_vectors = sum_replicas(
-        (part_out, scatter_weight(part_qkv), part_vectors)
-    )
+    out_rows, vector_size = part_out.shape[0], part_vectors.size
+    padded = jnp.pad(part_vectors.reshape(-1), (0, -vector_size % width)).reshape(-1, width)
+    joined, part_qkv = sum_replicas((jnp.concatenate([part_out, padded]), part_qkv))
+    part_out = joined[:out_rows]
+    part_vectors = joined[out_rows:].reshape(1, -1)[:, :vector_size]
     (
         own_query_b,
         own_value_b,

time: 609 us -> 556 us (0.913)
  other arithmetic: 116 us -> 90.2 us
  blocking collectives: 35.7 us -> 12.3 us
  matrix products: 146 us -> 139 us
    concatenate x1 -> x5, other arithmetic: 29 us -> 2.96 us  [the longest x1 1.7 us: shards(): jnp.concatenate([part_out, padded])]
    psum x1 -> x0, blocking collectives: 23.3 us -> none  [sum_replicas(): return lax.psum(parts, 'dp', axis_index_groups=same_core_groups())]
    psum x3, waiting for transfers between devices: 128 us -> 115 us  [sum_replicas(): return lax.psum(parts, 'dp', axis_index_groups=same_core_groups())]
    ppermute x5, waiting for transfers between devices: 33.7 us -> 43.6 us  [scatter_weight(): theirs = lax.ppermute(sent, 'fsdp', row_pairs(distance))]
    unnamed x168 -> x176, local copies, waits for them, and re-layouts: 31.1 us -> 35.1 us
  transfers between devices with their start and end apart: 26 -> 26, of which waited for: 7 -> 8; matrix products, arithmetic and copies ran while one was open for 38% -> 37% of each run, Pallas kernels for 0% -> 0%
where the time goes in v3:
time: 556 us; the launch traced here: 549 us
  waiting for transfers between devices  209 us (38%)
  matrix products  139 us (25%)
  other arithmetic  90.2 us (16%)
  local copies, waits for them, and re-layouts  67.2 us (12%)
  starting transfers between devices  16.4 us (3%)
  between operations  15.3 us (3%)
  blocking collectives  12.3 us (2%)
    psum x3, waiting for transfers between devices, sum_replicas(): return lax.psum(parts, 'dp', axis_index_groups=same_core_groups())  115 us
    ppermute x4, waiting for transfers between devices, gather_halves(): theirs = lax.ppermute(mine, 'fsdp', row_pairs(distance))  47.6 us
    ppermute x5, waiting for transfers between devices, scatter_weight(): theirs = lax.ppermute(sent, 'fsdp', row_pairs(distance))  43.6 us
    unnamed x176, local copies, waits for them, and re-layouts  35.1 us
    dot_general x4, matrix products, trans_right(): lax.dot_general(left, right, (((1,), (1,)), ((), ())), preferred_element_...  34.7 us
    dot_general x4, matrix products, product(): return jnp.dot(left, right, preferred_element_type=jnp.float32)  29.7 us
    dot_general x2, matrix products, attend_back(): jnp.einsum('gyx,uyx->ygu', gradient_context_rows, value_vectors, preferre...  22.2 us
    dot_general x4, matrix products, trans_left(): lax.dot_general(left, right, (((0,), (0,)), ((), ())), preferred_element_...  18 us
  transfers between devices with their start and end apart: 26, of which 8 were waited for; matrix products, arithmetic and copies ran while one was open for 37% of the time, Pallas kernels for 0%

profile of v3, /device:TPU:0, one launch (start us, length us, event | category | flops | bytes accessed | tf_op | source)
XLA Modules:
  0.0 549.1 jit_solution(2165354510023997149)
XLA Ops:
  19.3 12.3 %all-gather.1 = bf16[2,1,4608]{2,1,0:T(2,128)(2,1)S(1)} all-gather(bf16[1,1,4608]{2,1,0:T(2,128)(2,1)S(1)} %reshape.475), channel_id=2, replica_groups=mesh['fsdp'=2,'dp'=16] {'fsdp'}, dimensions={0}, use_global_device_ids=true | all-gather | bytes 27648 | tf_op jit(solution)/shard_map/all_gather | solution.py:148
  47.2 27.5 %collective-permute-done.2 = bf16[1,192,768]{2,1,0:T(8,128)(2,1)} collective-permute-done((bf16[1,192,768]{2,1,0:T(8,128)(2,1)S(1)}, bf16[1,192,768]{2,1,0:T(8,128)(2,1)}, u32[]{:S(2)}, u32[]{:S(2)}) %collective-permute-start.2) | collective-permute-done | bytes 294944 | tf_op jit(solution)/shard_map/ppermute | solution.py:134
  78.2 20.0 %collective-permute-done.6 = bf16[1,768,768]{2,1,0:T(8,128)(2,1)S(1)} collective-permute-done((bf16[1,768,768]{2,1,0:T(8,128)(2,1)S(1)}, bf16[1,768,768]{2,1,0:T(8,128)(2,1)S(1)}, u32[]{:S(2)}, u32[]{:S(2)}) %collective-permute-start.6) | collective-permute-done | bytes 1179680 | tf_op jit(solution)/shard_map/ppermute | solution.py:134
  102.3 5.2 fusion.18
  116.4 4.6 fusion.38
  144.4 17.4 %multiply_convert_fusion.3 = (bf16[1024,3072]{1,0:T(8,128)(2,1)S(1)}, f32[1024,3072]{1,0:T(8,128)}) fusion(f32[3072]{0:T(1024)S(1)} %reshape.458, bf16[768,3072]{1,0:T(8,128)(2,1)S(1)} %bitcast.237, f32[1024,768]{1,0:T(8,128)S(1)} %get-tuple-element.162, f32[768]{0:T(1024)S(1)} %reshape.457, f32[768]{0:T(1024)S(1)} %reshape.456, ...), kind=kOutput, calls=%fused_computation.15 | convolution fusion | flops 4908122112 | bytes 26765312 | tf_op jit(solution)/shard_map/dot_general | solution.py:16
  161.7 5.4 fusion.69
  173.8 5.8 %convolution_convert_fusion.1 = bf16[3072,768]{1,0:T(8,128)(2,1)S(1)} fusion(bf16[1024,3072]{1,0:T(8,128)(2,1)S(1)} %get-tuple-element.163, f32[1024,768]{1,0:T(8,128)S(1)} %get-tuple-element.94), kind=kOutput, calls=%fused_computation.34 | convolution fusion | flops 4834983936 | bytes 14155776 | tf_op jit(solution)/shard_map/dot_general | solution.py:20
  181.7 16.9 %multiply_convert_fusion.2 = bf16[1024,3072]{1,0:T(8,128)(2,1)S(1)} fusion(bf16[3072,768]{1,0:T(8,128)(2,1)} %bitcast.242, f32[1024,3072]{1,0:T(8,128)} %get-tuple-element.164, f32[3072]{0:T(1024)S(1)} %reshape.458, f32[1024,768]{1,0:T(8,128)S(1)} %get-tuple-element.94), kind=kOutput, calls=%fused_computation.14 | convolution fusion | flops 4920705024 | bytes 26750976 | tf_op jit(solution)/shard_map/dot_general | solution.py:26
  198.7 4.2 fusion.20
  202.9 6.7 %convolution_convert_fusion = bf16[768,3072]{1,0:T(8,128)(2,1)S(1)} fusion(bf16[1024,3072]{1,0:T(8,128)(2,1)S(1)} %multiply_convert_fusion.2, f32[1024,768]{1,0:T(8,128)S(1)} %get-tuple-element.162, f32[768]{0:T(1024)S(1)} %reshape.457, f32[768]{0:T(1024)S(1)} %reshape.456, f32[1024]{0:T(1024)S(1)} %add_rsqrt_fusion.1, f32[1024]{0:T(1024)S(1)} %broadcast_multiply_fusion.4), kind=kOutput, calls=%fused_computation.33 | convolution fusion | flops 4838129664 | bytes 14170112 | tf_op jit(solution)/shard_map/dot_general | solution.py:20
  214.5 6.8 %convolution_add_fusion = f32[1024,768]{1,0:T(8,128)} fusion(f32[1024,768]{1,0:T(8,128)S(1)} %copy-done.30, bf16[1024,3072]{1,0:T(8,128)(2,1)S(1)} %multiply_convert_fusion.2, bf16[768,3072]{1,0:T(8,128)(2,1)S(1)} %bitcast.240), kind=kOutput, calls=%fused_computation.92 | convolution fusion | flops 4832624640 | bytes 17301504 | tf_op jit(solution)/shard_map/dot_general | solution.py:26
  221.2 19.7 %collective-permute-done.9 = bf16[1,768,768]{2,1,0:T(8,128)(2,1)S(1)} collective-permute-done((bf16[1,768,768]{2,1,0:T(8,128)(2,1)S(1)}, bf16[1,768,768]{2,1,0:T(8,128)(2,1)S(1)}, u32[]{:S(2)}, u32[]{:S(2)}) %collective-permute-start.9) | collective-permute-done | bytes 1179680 | tf_op jit(solution)/shard_map/ppermute | solution.py:176
  259.1 4.9 collective-permute-done.13
  272.7 11.4 %multiply_reduce_fusion.1 = (f32[12,512]{1,0:T(8,128)S(1)}, f32[12,512,512]{1,2,0:T(8,128)}) fusion(f32[12,512,512]{1,2,0:T(8,128)} %copy-done.1, f32[12,512]{1,0:T(8,128)S(1)} %log_add_fusion.1, bf16[512,12,64]{0,2,1:T(8,128)(2,1)S(1)} %bitcast.223, bf16[512,12,64]{0,2,1:T(8,128)(2,1)} %bitcast.250), kind=kOutput, calls=%fused_computation.12 | convolution fusion | flops 412084224 | bytes 26787840 | tf_op jit(solution)/shard_map/gyx,uyx->ygu/dot_general | solution.py:76
  285.9 7.0 %multiply_convert_fusion.1 = bf16[12,512,512]{1,2,0:T(8,128)(2,1)S(1)} fusion(f32[12,512,512]{1,2,0:T(8,128)} %get-tuple-element.168, f32[12,512,512]{1,2,0:T(8,128)S(1)} %bitcast.216, f32[12,512]{1,0:T(8,128)S(1)} %get-tuple-element.167, f32[12,512]{1,0:T(8,128)S(1)} %log_add_fusion.1), kind=kLoop, calls=%fused_computation.11 | loop fusion | flops 12582912 | bytes 31506432 | tf_op jit(solution)/shard_map/convert_element_type | solution.py:80
  298.1 4.9 fusion.36
  303.0 7.5 %fusion.33 = bf16[512,12,64]{0,2,1:T(8,128)(2,1)} fusion(bf16[512,12,64]{0,2,1:T(8,128)(2,1)S(1)} %bitcast.224, f32[12,512,512]{1,2,0:T(8,128)} %copy-done.1, f32[12,512]{1,0:T(8,128)S(1)} %log_add_fusion.1), kind=kOutput, calls=%fused_computation.108 | convolution fusion | flops 409337856 | bytes 14180352 | tf_op jit(solution)/shard_map/ygu,gyp->uyp/dot_general | solution.py:93
  313.3 10.8 %multiply_reduce_fusion = (f32[12,512]{1,0:T(8,128)S(1)}, f32[12,512,512]{1,2,0:T(8,128)}) fusion(f32[12,512,512]{1,2,0:T(8,128)} %copy-done, f32[12,512]{1,0:T(8,128)S(1)} %log_add_fusion, bf16[512,12,64]{0,2,1:T(8,128)(2,1)S(1)} %bitcast.221, bf16[512,12,64]{0,2,1:T(8,128)(2,1)} %bitcast.248), kind=kOutput, calls=%fused_computation.9 | convolution fusion | flops 412084224 | bytes 26787840 | tf_op jit(solution)/shard_map/gyx,uyx->ygu/dot_general | solution.py:76
  326.5 7.1 %multiply_convert_fusion = bf16[12,512,512]{1,2,0:T(8,128)(2,1)S(1)} fusion(f32[12,512,512]{1,2,0:T(8,128)} %get-tuple-element.170, f32[12,512,512]{1,2,0:T(8,128)S(1)} %bitcast.214, f32[12,512]{1,0:T(8,128)S(1)} %get-tuple-element.169, f32[12,512]{1,0:T(8,128)S(1)} %log_add_fusion), kind=kLoop, calls=%fused_computation.8 | loop fusion | flops 12582912 | bytes 31506432 | tf_op jit(solution)/shard_map/convert_element_type | solution.py:80
  379.5 19.0 %collective-permute-done.15 = bf16[1,192,2304]{2,1,0:T(8,128)(2,1)S(1)} collective-permute-done((bf16[1,192,2304]{2,1,0:T(8,128)(2,1)S(1)}, bf16[1,192,2304]{2,1,0:T(8,128)(2,1)S(1)}, u32[]{:S(2)}, u32[]{:S(2)}) %collective-permute-start.15) | collective-permute-done | bytes 884768 | tf_op jit(solution)/shard_map/ppermute | solution.py:176
  399.6 41.8 %all-reduce.7.cloned.1.call-done = bf16[192,3072]{1,0:T(8,128)(2,1)} async-done(((bf16[192,3072]{1,0:T(8,128)(2,1)}), bf16[192,3072]{1,0:T(8,128)(2,1)}) %all-reduce.7.cloned.1.call-update) | async-done | bytes 1179664 | tf_op jit(solution)/shard_map/psum | solution.py:183
  441.9 8.3 %convolution_add_fusion.1 = f32[1024,768]{1,0:T(8,128)} fusion(f32[1024,768]{1,0:T(8,128)} %copy-done.32, bf16[1024,2304]{0,1:T(8,128)(2,1)} %copy-done.3, bf16[768,2304]{1,0:T(8,128)(2,1)S(1)} %bitcast.244), kind=kOutput, calls=%fused_computation.93 | convolution fusion | flops 3624665088 | bytes 14548992 | tf_op jit(solution)/shard_map/dot_general | solution.py:26
  459.6 73.3 %all-reduce.9.cloned.1.call-done = (bf16[192,2304]{1,0:T(8,128)(2,1)}, bf16[195,768]{1,0:T(8,128)(2,1)}) async-done(((bf16[192,2304]{1,0:T(8,128)(2,1)}, bf16[195,768]{1,0:T(8,128)(2,1)}), (bf16[192,2304]{1,0:T(8,128)(2,1)}, bf16[195,768]{1,0:T(8,128)(2,1)})) %all-reduce.9.cloned.1.call-update) | async-done | bytes 1184272 | tf_op jit(solution)/shard_map/psum | solution.py:183
  (359 shorter events, 185.3 us)
Async XLA Ops:
  7.2 332.6 %all-reduce.5.cloned.1.call-start = ((), (), s32[]{:S(2)}) async-start(), calls=%async_computation | async-start | bytes 2359296 | tf_op jit(solution)/shard_map/psum | solution.py:183
  8.6 26.4 %collective-permute-start = (bf16[1,192,2304]{2,1,0:T(8,128)(2,1)S(1)}, bf16[1,192,2304]{2,1,0:T(8,128)(2,1)}, u32[]{:S(2)}, u32[]{:S(2)}) collective-permute-start(bf16[1,192,2304]{2,1,0:T(8,128)(2,1)S(1)} %fusion.46), channel_id=1, source_target_pairs={{0,16},{16,0},{1,17},{17,1},{2,18},{18,2},{3,19},{19,3},{4,20},{20... | collective-permute-start | bytes 2654216 | tf_op jit(solution)/shard_map/ppermute | solution.py:134
  39.2 37.6 %collective-permute-start.4 = (bf16[1,192,3072]{2,1,0:T(8,128)(2,1)}, bf16[1,192,3072]{2,1,0:T(8,128)(2,1)S(1)}, u32[]{:S(2)}, u32[]{:S(2)}) collective-permute-start(bf16[1,192,3072]{2,1,0:T(8,128)(2,1)} %dynamic-slice_bitcast_fusion.4), channel_id=1, source_target_pairs={{0,16},{16,0},{1,17},{17,1},{2,18},{18,2},{3,19},{19,3},{4,20},{20... | collective-permute-start | bytes 3538952 | tf_op jit(solution)/shard_map/ppermute | solution.py:134
  42.1 32.6 %collective-permute-start.2 = (bf16[1,192,768]{2,1,0:T(8,128)(2,1)S(1)}, bf16[1,192,768]{2,1,0:T(8,128)(2,1)}, u32[]{:S(2)}, u32[]{:S(2)}) collective-permute-start(bf16[1,192,768]{2,1,0:T(8,128)(2,1)S(1)} %dynamic-slice_bitcast_fusion.6), channel_id=1, source_target_pairs={{0,16},{16,0},{1,17},{17,1},{2,18},{18,2},{3,19},{19,3},{4,20},{20... | collective-permute-start | bytes 884744 | tf_op jit(solution)/shard_map/ppermute | solution.py:134
  43.8 56.6 %collective-permute-start.1 = (bf16[2,192,2304]{2,1,0:T(8,128)(2,1)}, bf16[2,192,2304]{2,1,0:T(8,128)(2,1)S(1)}, u32[]{:S(2)}, u32[]{:S(2)}) collective-permute-start(bf16[2,192,2304]{2,1,0:T(8,128)(2,1)} %pad_maximum_fusion.8), channel_id=1, source_target_pairs={{0,1},{1,0},{2,3},{3,2},{4,5},{5,4},{6,7},{7,6},{8,9},{9,8},{10,11... | collective-permute-start | bytes 5308424 | tf_op jit(solution)/shard_map/ppermute | solution.py:140
  45.4 52.9 %collective-permute-start.6 = (bf16[1,768,768]{2,1,0:T(8,128)(2,1)S(1)}, bf16[1,768,768]{2,1,0:T(8,128)(2,1)S(1)}, u32[]{:S(2)}, u32[]{:S(2)}) collective-permute-start(bf16[1,768,768]{2,1,0:T(8,128)(2,1)S(1)} %dynamic-slice_bitcast_fusion.3), channel_id=1, source_target_pairs={{0,16},{16,0},{1,17},{17,1},{2,18},{18,2},{3,19},{19,3},{4,20},{20... | collective-permute-start | bytes 3538952 | tf_op jit(solution)/shard_map/ppermute | solution.py:134
  76.8 54.6 %collective-permute-start.3 = (bf16[2,192,768]{2,1,0:T(8,128)(2,1)}, bf16[2,192,768]{2,1,0:T(8,128)(2,1)}, u32[]{:S(2)}, u32[]{:S(2)}) collective-permute-start(bf16[2,192,768]{2,1,0:T(8,128)(2,1)} %pad_maximum_fusion.15), channel_id=1, source_target_pairs={{0,1},{1,0},{2,3},{3,2},{4,5},{5,4},{6,7},{7,6},{8,9},{9,8},{10,11... | collective-permute-start | bytes 1769480 | tf_op jit(solution)/shard_map/ppermute | solution.py:140
  77.6 53.7 %collective-permute-start.5 = (bf16[2,192,3072]{2,1,0:T(8,128)(2,1)S(1)}, bf16[2,192,3072]{2,1,0:T(8,128)(2,1)}, u32[]{:S(2)}, u32[]{:S(2)}) collective-permute-start(bf16[2,192,3072]{2,1,0:T(8,128)(2,1)S(1)} %pad_maximum_fusion.4), channel_id=1, source_target_pairs={{0,1},{1,0},{2,3},{3,2},{4,5},{5,4},{6,7},{7,6},{8,9},{9,8},{10,11... | collective-permute-start | bytes 7077896 | tf_op jit(solution)/shard_map/ppermute | solution.py:140
  100.4 31.0 %collective-permute-start.7 = (bf16[2,768,768]{2,1,0:T(8,128)(2,1)}, bf16[2,768,768]{2,1,0:T(8,128)(2,1)}, u32[]{:S(2)}, u32[]{:S(2)}) collective-permute-start(bf16[2,768,768]{2,1,0:T(8,128)(2,1)} %pad_maximum_fusion.5), channel_id=1, source_target_pairs={{0,1},{1,0},{2,3},{3,2},{4,5},{5,4},{6,7},{7,6},{8,9},{9,8},{10,11... | collective-permute-start | bytes 7077896 | tf_op jit(solution)/shard_map/ppermute | solution.py:140
  181.2 17.5 %collective-permute-start.8 = (bf16[2,768,768]{2,1,0:T(8,128)(2,1)}, bf16[2,768,768]{2,1,0:T(8,128)(2,1)}, u32[]{:S(2)}, u32[]{:S(2)}) collective-permute-start(bf16[2,768,768]{2,1,0:T(8,128)(2,1)} %dynamic-slice_bitcast_fusion.1), channel_id=1, source_target_pairs={{0,1},{1,0},{2,3},{3,2},{4,5},{5,4},{6,7},{7,6},{8,9},{9,8},{10,11... | collective-permute-start | bytes 7077896 | tf_op jit(solution)/shard_map/ppermute | solution.py:165
  211.2 53.7 %collective-permute-start.10 = (bf16[2,192,3072]{2,1,0:T(8,128)(2,1)}, bf16[2,192,3072]{2,1,0:T(8,128)(2,1)}, u32[]{:S(2)}, u32[]{:S(2)}) collective-permute-start(bf16[2,192,3072]{2,1,0:T(8,128)(2,1)} %dynamic-slice_bitcast_fusion), channel_id=1, source_target_pairs={{0,1},{1,0},{2,3},{3,2},{4,5},{5,4},{6,7},{7,6},{8,9},{9,8},{10,11... | collective-permute-start | bytes 7077896 | tf_op jit(solution)/shard_map/ppermute | solution.py:165
  213.0 27.9 %collective-permute-start.9 = (bf16[1,768,768]{2,1,0:T(8,128)(2,1)S(1)}, bf16[1,768,768]{2,1,0:T(8,128)(2,1)S(1)}, u32[]{:S(2)}, u32[]{:S(2)}) collective-permute-start(bf16[1,768,768]{2,1,0:T(8,128)(2,1)S(1)} %constant_dynamic-slice_fusion.4), channel_id=1, source_target_pairs={{0,16},{16,0},{1,17},{17,1},{2,18},{18,2},{3,19},{19,3},{4,20},{20... | collective-permute-start | bytes 3538952 | tf_op jit(solution)/shard_map/ppermute | solution.py:176
  251.3 190.1 %all-reduce.7.cloned.1.call-start = ((), (), s32[]{:S(2)}) async-start(), calls=%async_computation.1 | async-start | bytes 2359296 | tf_op jit(solution)/shard_map/psum | solution.py:183
  255.0 9.1 %collective-permute-start.13 = (bf16[1,192,768]{2,1,0:T(8,128)(2,1)S(1)}, bf16[1,192,768]{2,1,0:T(8,128)(2,1)S(1)}, u32[]{:S(2)}, u32[]{:S(2)}) collective-permute-start(bf16[1,192,768]{2,1,0:T(8,128)(2,1)S(1)} %constant_dynamic-slice_fusion.2), channel_id=1, source_target_pairs={{0,16},{16,0},{1,17},{17,1},{2,18},{18,2},{3,19},{19,3},{4,20},{20... | collective-permute-start | bytes 884744 | tf_op jit(solution)/shard_map/ppermute | solution.py:176
  268.6 41.9 %collective-permute-start.11 = (bf16[1,192,3072]{2,1,0:T(8,128)(2,1)}, bf16[1,192,3072]{2,1,0:T(8,128)(2,1)}, u32[]{:S(2)}, u32[]{:S(2)}) collective-permute-start(bf16[1,192,3072]{2,1,0:T(8,128)(2,1)} %constant_dynamic-slice_fusion.3), channel_id=1, source_target_pairs={{0,16},{16,0},{1,17},{17,1},{2,18},{18,2},{3,19},{19,3},{4,20},{20... | collective-permute-start | bytes 3538952 | tf_op jit(solution)/shard_map/ppermute | solution.py:176
  348.5 26.2 %collective-permute-start.14 = (bf16[2,192,2304]{2,1,0:T(8,128)(2,1)}, bf16[2,192,2304]{2,1,0:T(8,128)(2,1)}, u32[]{:S(2)}, u32[]{:S(2)}) collective-permute-start(bf16[2,192,2304]{2,1,0:T(8,128)(2,1)} %dynamic-slice_bitcast_fusion.2), channel_id=1, source_target_pairs={{0,1},{1,0},{2,3},{3,2},{4,5},{5,4},{6,7},{7,6},{8,9},{9,8},{10,11... | collective-permute-start | bytes 5308424 | tf_op jit(solution)/shard_map/ppermute | solution.py:165
  360.8 172.1 %all-reduce.9.cloned.1.call-start = ((), (), s32[]{:S(2)}) async-start(), calls=%async_computation.2 | async-start | bytes 2383872 | tf_op jit(solution)/shard_map/psum | solution.py:183
  374.2 3.2 collective-permute-start.17
  376.7 21.7 %collective-permute-start.15 = (bf16[1,192,2304]{2,1,0:T(8,128)(2,1)S(1)}, bf16[1,192,2304]{2,1,0:T(8,128)(2,1)S(1)}, u32[]{:S(2)}, u32[]{:S(2)}) collective-permute-start(bf16[1,192,2304]{2,1,0:T(8,128)(2,1)S(1)} %constant_dynamic-slice_fusion.1), channel_id=1, source_target_pairs={{0,16},{16,0},{1,17},{17,1},{2,18},{18,2},{3,19},{19,3},{4,20},{20... | collective-permute-start | bytes 2654216 | tf_op jit(solution)/shard_map/ppermute | solution.py:176
  378.0 72.2 %collective-permute-start.18 = (bf16[1,1,2304]{2,1,0:T(2,128)(2,1)}, bf16[1,1,2304]{2,1,0:T(2,128)(2,1)S(1)}, u32[]{:S(2)}, u32[]{:S(2)}) collective-permute-start(bf16[1,1,2304]{2,1,0:T(2,128)(2,1)} %constant_dynamic-slice_fusion), channel_id=1, source_target_pairs={{0,16},{16,0},{1,17},{17,1},{2,18},{18,2},{3,19},{19,3},{4,20},{20... | collective-permute-start | bytes 13832 | tf_op jit(solution)/shard_map/ppermute | solution.py:176
  441.4 10.7 %collective-permute-start.22 = (bf16[768,768]{1,0:T(8,128)(2,1)}, bf16[768,768]{1,0:T(8,128)(2,1)}, u32[]{:S(2)}, u32[]{:S(2)}) collective-permute-start(bf16[768,768]{1,0:T(8,128)(2,1)} %all-reduce.5.cloned.1.call-done), channel_id=1, source_target_pairs={{0,1},{1,0},{2,3},{3,2},{4,5},{5,4},{6,7},{7,6},{8,9},{9,8},{10,11... | collective-permute-start | bytes 3538952 | tf_op jit(solution)/shard_map/ppermute | solution.py:187
  441.4 12.7 %collective-permute-start.21 = (bf16[192,3072]{1,0:T(8,128)(2,1)}, bf16[192,3072]{1,0:T(8,128)(2,1)}, u32[]{:S(2)}, u32[]{:S(2)}) collective-permute-start(bf16[192,3072]{1,0:T(8,128)(2,1)} %all-reduce.7.cloned.1.call-done), channel_id=1, source_target_pairs={{0,1},{1,0},{2,3},{3,2},{4,5},{5,4},{6,7},{7,6},{8,9},{9,8},{10,11... | collective-permute-start | bytes 3538952 | tf_op jit(solution)/shard_map/ppermute | solution.py:187
  533.7 3.5 collective-permute-start.20
  537.0 2.7 collective-permute-start.16
  (79 other events, 615.1 us)
Sparse Core Ops, SparseCore 0:
  251.4 81.3 all-reduce.4
  361.0 80.3 all-reduce.6
  452.1 80.7 all-reduce.8
